TPU v7x, 128 devices: a whole 4x4x4 slice. The times are simulated.
128 devices in a mesh: slab: 32 (over x, y, core), sub: 4 (over z).
Axes of the slice: x: 4, y: 4, z: 4, core: 2. Of those that a mesh axis runs over, the one named last changes fastest.
Arguments:
- load_values: float32 [3, 128, 32, 256], P(None, 'slab', 'sub'), may hold values from -6 to 6
- load_mask: int32 [128, 32, 256], P('slab', 'sub'), may hold values 0 or 1
- fixed_mask: int32 [128, 32, 256], P('slab', 'sub'), may hold values 0 or 1
- frequencies: float32 [3, 128], replicated, may hold values from -24 to 24
- weight_in: bfloat16 [256, 512], replicated, may hold values from -0.375 to 0.375
- weight_mid: bfloat16 [512, 512], replicated, may hold values from -0.25 to 0.25
- weight_out: bfloat16 [512], replicated, may hold values from -0.25 to 0.25
Outputs:
- displacement: float32 [3, 128, 32, 256], P(None, 'slab', 'sub')
- density: float32 [128, 32, 256], P('slab', 'sub')
- grad_weight_in: float32 [256, 512], replicated
- grad_weight_mid: float32 [512, 512], replicated
- grad_weight_out: float32 [512], replicated
All inputs are finite; a program needn't handle non-finite values. No bound on the sum of `load_mask` or of `fixed_mask` on one device may be relied on, other than what follows from the above.
Results may differ from a plain program's by a relative error of at most 0.00055.
Values sent between devices are 32-bit elements; how exact they have to be, the bound alone decides.
No kernel may reach another device: no remote copies, remote signals or barrier semaphores. Data moves between devices by JAX's collectives and lax.ppermute only.
A program may use at most 256 MiB of HBM per device.

v0:
```python
import functools
import itertools
import math

import jax
import jax.numpy as jnp
import numpy as np
from jax import lax
from jax.experimental import pallas as pl
from jax.experimental.pallas import tpu as pltpu
from jax.sharding import Mesh
from jax.sharding import PartitionSpec as P

ITERS = 3
SLAB = ("x", "y", "c")
CHIPS = ("x", "y", "z")
ALL = ("x", "y", "c", "z")
BF = jnp.bfloat16
F32 = jnp.float32

two_pi = 2.0 * math.pi
emin = 0.001
penalty = 4.0
vol_target = 0.3
ROWS = 16
corner_list = list(itertools.product((0, 1), repeat=3))
LAST = (((1,), (1,)), ((), ()))


def hex_stiffness():
    poisson = 0.3
    lame_first = poisson / ((1.0 + poisson) * (1.0 - 2.0 * poisson))
    lame_second = 0.5 / (1.0 + poisson)
    elastic = np.zeros((6, 6))
    elastic[:3, :3] = lame_first
    for axis_number in range(3):
        elastic[axis_number, axis_number] += 2.0 * lame_second
        elastic[axis_number + 3, axis_number + 3] = lame_second
    gauss_points = [0.5 - 0.5 / math.sqrt(3.0), 0.5 + 0.5 / math.sqrt(3.0)]
    matrix = np.zeros((24, 24))
    for location in itertools.product(gauss_points, repeat=3):
        strain = np.zeros((6, 24))
        for corner_number, corner in enumerate(corner_list):
            factors = [
                location[axis] if corner[axis] == 1 else 1.0 - location[axis] for axis in range(3)
            ]
            slopes = [1.0 if corner[axis] == 1 else -1.0 for axis in range(3)]
            derivative = [
                slopes[0] * factors[1] * factors[2],
                factors[0] * slopes[1] * factors[2],
                factors[0] * factors[1] * slopes[2],
            ]
            column = 3 * corner_number
            for axis in range(3):
                strain[axis, column + axis] = derivative[axis]
            strain[3, column + 1] = derivative[2]
            strain[3, column + 2] = derivative[1]
            strain[4, column + 0] = derivative[2]
            strain[4, column + 2] = derivative[0]
            strain[5, column + 0] = derivative[1]
            strain[5, column + 1] = derivative[0]
        matrix += strain.T @ elastic @ strain / 8.0
    return matrix


def modal_stiffness():
    table = hex_stiffness()
    change = np.zeros((24, 24))
    for row, wave in enumerate(corner_list):
        for column, corner in enumerate(corner_list):
            sign = np.prod([1.0 if c == 1 else -1.0 for w, c in zip(wave, corner) if w == 1])
            for d in range(3):
                change[3 * row + d, 3 * column + d] = sign
    modal = change @ table @ change.T / 64.0
    blocks = []
    for parity in corner_list:
        waves = [tuple(parity[a] ^ (a == d) for a in range(3)) for d in range(3)]
        index = [3 * corner_list.index(wave) + d for d, wave in enumerate(waves)]
        block = modal[np.ix_(index, index)]
        blocks.append((waves, np.where(np.abs(block) < 1e-9, 0.0, block)))
    return blocks


BLOCKS = modal_stiffness()


def lane_mask(shape, lane):
    return lax.broadcasted_iota(jnp.int32, shape, len(shape) - 1) == lane


def plane_modes(plane, rows):
    size = plane.shape[-1]
    ahead = jnp.where(lane_mask(plane.shape, size - 1), 0.0, pltpu.roll(plane, size - 1, 1))
    modes = {}
    for wave_z, part in ((0, plane + ahead), (1, ahead - plane)):
        following = pltpu.roll(part, ROWS - 1, 0)
        modes[0, wave_z] = (part + following)[:rows]
        modes[1, wave_z] = (following - part)[:rows]
    return modes


def element_modes(lower, upper):
    found = []
    for low, high in zip(lower, upper):
        modes = {}
        for key in low:
            modes[(0,) + key] = low[key] + high[key]
            modes[(1,) + key] = high[key] - low[key]
        found.append(modes)
    return found


def modal_forces(modes):
    for waves, block in BLOCKS:
        values = [modes[d][waves[d]] for d in range(3)]
        for d in range(3):
            total = None
            for other in range(3):
                if block[d, other] != 0.0:
                    term = np.float32(block[d, other]) * values[other]
                    total = term if total is None else total + term
            if total is not None:
                yield d, waves[d], values[d], total


def energy_of(modes):
    total = None
    for _, _, value, force in modal_forces(modes):
        total = value * force if total is None else total + value * force
    return total


def node_plane(gathered):
    parts = []
    for wave_z in (0, 1):
        even, odd = gathered[0, wave_z], gathered[1, wave_z]
        parts.append((even - odd) + pltpu.roll(even + odd, 1, 0))
    behind = pltpu.roll(parts[0] + parts[1], 1, 1)
    return (parts[0] - parts[1]) + jnp.where(lane_mask(behind.shape, 0), 0.0, behind)


def operator_planes(planes, stiff, free):
    modes = [[plane_modes(component, ROWS) for component in plane] for plane in planes]
    gathered = [[{} for _ in range(3)] for _ in planes]
    for e in range(len(planes) - 1):
        forces = [{} for _ in range(3)]
        for d, wave, _, force in modal_forces(element_modes(modes[e], modes[e + 1])):
            forces[d][wave] = force * stiff[e]
        for d in range(3):
            for key in itertools.product((0, 1), repeat=2):
                even, odd = forces[d].get((0,) + key), forces[d].get((1,) + key)
                for node, sign in ((e, -1), (e + 1, 1)):
                    if even is None:
                        term = odd if sign == 1 else -odd
                    else:
                        term = even + odd if sign == 1 else even - odd
                    held = gathered[node][d]
                    held[key] = term if key not in held else held[key] + term
    return [
        [node_plane(gathered[n][d]) * free[n - 1] for d in range(3)]
        for n in range(1, len(planes) - 1)
    ]


def krylov_kernel(loads, stiff, density, first, second, sums):
    planes = loads.shape[1]
    cells = planes - 5
    stiff_planes = [stiff[e] for e in range(planes - 1)]
    force = [[loads[d, p] for d in range(3)] for p in range(planes)]
    free = [loads[3, p] for p in range(planes)]
    image = operator_planes(force, stiff_planes, free[1:-1])
    twice = operator_planes(image, stiff_planes[1:-1], free[2:-2])
    own = (force[2 : 2 + cells], image[1 : 1 + cells], twice[:cells])
    rows = density.shape[1]

    def dot(left, right):
        total = None
        for p in range(cells):
            for d in range(3):
                term = left[p][d][:rows] * right[p][d][:rows]
                total = term if total is None else total + term
        return total

    totals = [dot(own[k // 2], own[(k + 1) // 2]) for k in range(2 * ITERS - 1)]
    modes = [[plane_modes(component, rows) for component in plane] for plane in twice]
    last = None
    volume = None
    for e in range(cells):
        term = stiff_planes[2 + e][:rows] * energy_of(element_modes(modes[e], modes[e + 1]))
        last = term if last is None else last + term
        volume = density[e] if volume is None else volume + density[e]
    totals += [last, volume]
    row_number = lax.broadcasted_iota(jnp.int32, sums.shape[1:], 0)
    result = jnp.zeros(sums.shape[1:], F32)
    for k, total in enumerate(totals):
        scalar = jnp.sum(jnp.sum(total, axis=0, keepdims=True), axis=1, keepdims=True)
        result = jnp.where(row_number == k, scalar, result)
    sums[...] = jnp.broadcast_to(result[None], sums.shape)
    for p in range(cells + 1):
        for d in range(3):
            first[d, p] = image[1 + p][d]
            second[d, p] = twice[p][d]


def krylov_steps(moments):
    mean = moments[1] / moments[0]
    powers = [None, mean]
    for k in range(2, 2 * ITERS):
        powers.append(powers[-1] * mean)
    scaled = [moments[k] / moments[0] / powers[k] if k else 1.0 for k in range(2 * ITERS)]

    def product(left, right, shift):
        return sum(
            left[i] * right[j] * scaled[i + j + shift]
            for i in range(len(left))
            for j in range(len(right))
        )

    solution = [0.0] * ITERS
    residual = [1.0]
    direction = [1.0]
    norm_now = scaled[0]
    work = 0.0
    for iteration in range(ITERS):
        alpha = norm_now / product(direction, direction, 1)
        work = work + alpha * norm_now
        solution = [
            solution[i] + (alpha * direction[i] if i < len(direction) else 0.0)
            for i in range(ITERS)
        ]
        if iteration + 1 < ITERS:
            image = [0.0] + direction
            residual = [
                (residual[i] if i < len(residual) else 0.0) - alpha * image[i]
                for i in range(len(image))
            ]
            norm_next = product(residual, residual, 0)
            beta = norm_next / norm_now
            direction = [
                residual[i] + (beta * direction[i] if i < len(direction) else 0.0)
                for i in range(len(residual))
            ]
            norm_now = norm_next
    factors = [solution[i] / powers[i + 1] for i in range(ITERS)]
    return factors, work * moments[0] / mean


def energy_kernel(elements, parts, loads, first, second, density, solution, slope):
    totals = jnp.sum(parts[...], axis=0)
    rows_of = [totals[k : k + 1, :] for k in range(2 * ITERS + 1)]
    factors, compliance = krylov_steps(rows_of[: 2 * ITERS])
    volume = rows_of[2 * ITERS]
    constant = 2.0 * penalty * (volume / elements - vol_target) / elements
    scale = -3.0 * (1.0 - emin) / compliance
    wide = [jnp.concatenate([value, value], axis=1) for value in factors + [scale, constant]]
    cells, rows, _ = density.shape
    modes = []
    for p in range(cells + 1):
        plane = []
        for d in range(3):
            value = wide[0] * loads[d, 2 + p] + wide[1] * first[d, p] + wide[2] * second[d, p]
            if p < cells:
                solution[d, p] = value[:rows]
            plane.append(plane_modes(value, rows))
        modes.append(plane)
    for e in range(cells):
        energy = energy_of(element_modes(modes[e], modes[e + 1]))
        held = density[e]
        slope[e] = (wide[3] * held * held * energy + wide[4]) * held * (1.0 - held)


def gated(half):
    up = 1.0 + jnp.tanh(half)
    value = half * up
    return value, up + value * (2.0 - up)


def features_of(x_cos, x_sin, z_cos, z_sin, column):
    cos = x_cos[0, :, column : column + 1]
    sin = x_sin[0, :, column : column + 1]
    return jnp.concatenate([z_cos * cos - z_sin * sin, z_sin * cos + z_cos * sin], 0).astype(BF)


def forward_kernel(
    x_cos, x_sin, z_cos, z_sin, w_in, w_mid, w_out, w_row,
    density, stiff, hidden_in, slope_mid, slope_in, hidden_mid, *, width,
):
    columns, size = density.shape[1:]
    step = pl.program_id(0)
    for g in range(columns // width):
        picked = [
            features_of(x_cos, x_sin, z_cos[...], z_sin[...], g * width + q) for q in range(width)
        ]
        features = jnp.concatenate(picked, 1)
        span = width * size
        place = pl.ds(pl.multiple_of(step * (columns * size) + g * span, span), span)
        value, slope = gated(jnp.dot(w_in[...], features, preferred_element_type=F32))
        value = value.astype(BF)
        hidden_in[:, place] = value
        slope_in[:, place] = slope.astype(BF)
        value, slope = gated(jnp.dot(w_mid[...], value, preferred_element_type=F32))
        value = value.astype(BF)
        hidden_mid[:, place] = value
        slope_mid[:, place] = (w_out[...] * slope).astype(BF)
        logits = jnp.dot(w_row[...], value, preferred_element_type=F32)[:1]
        held = 0.5 * jnp.tanh(0.5 * logits) + 0.5
        for q in range(width):
            part = held[:, q * size : (q + 1) * size]
            density[0, g * width + q : g * width + q + 1, :] = part
            stiff[0, g * width + q : g * width + q + 1, :] = emin + (1.0 - emin) * (
                part * part * part
            )


def back_kernel(w_mid, slope_mid, slope_in, back, *, span):
    place = pl.ds(pl.multiple_of(pl.program_id(0) * span, span), span)
    product = jnp.dot(w_mid[...], slope_mid[:, place], preferred_element_type=F32)
    back[:, place] = (product * slope_in[:, place].astype(F32)).astype(BF)


def gradient_kernel(
    slope, x_cos, x_sin, z_cos, z_sin, hidden_in, slope_mid, back, hidden_mid,
    grads, grad_out, running, *, steps,
):
    step = pl.program_id(0)

    @pl.when(step == 0)
    def _():
        grads[...] = jnp.zeros_like(grads)
        running[...] = jnp.zeros_like(running)

    columns, size = slope.shape[1:]
    span = columns * size
    picked = []
    for q in range(columns):
        features = features_of(x_cos, x_sin, z_cos[...], z_sin[...], q).astype(F32)
        picked.append((features * slope[0, q : q + 1, :]).astype(BF))
    features = jnp.concatenate(picked, 1)
    place = pl.ds(pl.multiple_of(step * span, span), span)
    row = jnp.concatenate([slope[0, q : q + 1, :] for q in range(columns)], 1)
    hidden = (hidden_in[:, place].astype(F32) * row).astype(BF)
    mid = lax.dot_general(hidden, slope_mid[:, place], LAST, preferred_element_type=F32)
    first = lax.dot_general(features, back[:, place], LAST, preferred_element_type=F32)
    height = mid.shape[0]
    for k in range(grads.shape[0]):
        grads[k, :height, :] += mid[:, k * 128 : (k + 1) * 128]
        grads[k, height:, :] += first[:, k * 128 : (k + 1) * 128]
    product = hidden_mid[:, place].astype(F32) * row
    total = product[:, :128]
    for k in range(1, span // 128):
        total = total + product[:, k * 128 : (k + 1) * 128]
    running[...] += total

    @pl.when(step == steps - 1)
    def _():
        line = jnp.sum(running[...].T, axis=0, keepdims=True)
        for k in range(grad_out.shape[0]):
            grad_out[k : k + 1, :] = line[:, k * 128 : (k + 1) * 128]


WHOLE = pl.BlockSpec(memory_space=pltpu.VMEM)


def fixed(shape):
    return pl.BlockSpec(shape, lambda i: (0,) * len(shape))


def in_vmem(array):
    return pltpu.with_memory_space_constraint(array, pltpu.VMEM)


def params(mebibytes):
    return pltpu.CompilerParams(vmem_limit_bytes=mebibytes << 20)


def shifted(block, axis, distance):
    size = lax.axis_size(axis)
    route = [(i, (i + distance) % size) for i in range(size)]
    got = lax.ppermute(block, axis, route)
    at_end = lax.axis_index(axis) == (0 if distance == 1 else size - 1)
    return jnp.where(at_end, 0.0, got)


def with_rows(block, before, after):
    dim = block.ndim - 2
    size = block.shape[dim]
    behind = shifted(lax.slice_in_dim(block, size - before, size, axis=dim), "z", 1)
    ahead = shifted(lax.slice_in_dim(block, 0, after, axis=dim), "z", -1)
    space = block.shape[:dim] + (ROWS - size - before - after,) + block.shape[dim + 1 :]
    return jnp.concatenate([block, ahead, jnp.zeros(space, F32), behind], axis=dim)


def with_planes(block, before, after):
    dim = block.ndim - 3
    size = block.shape[dim]
    behind = shifted(lax.slice_in_dim(block, size - before, size, axis=dim), SLAB, 1)
    ahead = shifted(lax.slice_in_dim(block, 0, after, axis=dim), SLAB, -1)
    return jnp.concatenate([behind, block, ahead], axis=dim)


def summed_grads(grads, grad_out):
    chips = lax.axis_size(CHIPS)
    core = lax.axis_index("c")
    swap = [(0, 1), (1, 0)]
    halves = grads.reshape(2, chips, -1, 128)
    height = halves.shape[2]
    mine = lax.dynamic_index_in_dim(halves, core, 0, keepdims=False)
    other = lax.dynamic_index_in_dim(halves, 1 - core, 0, keepdims=False)
    half = mine + lax.ppermute(other, "c", swap)
    share = jnp.sum(lax.all_to_all(half, CHIPS, 0, 0), axis=0)
    share = jnp.concatenate([share, grad_out], axis=0)
    half = lax.all_to_all(jnp.broadcast_to(share[None], (chips,) + share.shape), CHIPS, 0, 0)
    out_half = jnp.sum(half[:, height:], axis=0)
    half = half[:, :height]
    away = lax.ppermute(half, "c", swap)
    out_away = lax.ppermute(out_half, "c", swap)
    first = jnp.where(core == 0, half, away)
    second = jnp.where(core == 0, away, half)
    return jnp.stack([first, second]).reshape(grads.shape), out_half + out_away


def on_device(load_values, load_mask, fixed_mask, frequencies, weight_in, weight_mid, weight_out):
    cells_x, cells_y, cells_z = fixed_mask.shape
    grid_cells = (cells_x * lax.axis_size(SLAB), cells_y * lax.axis_size("z"), cells_z)
    elements_total = grid_cells[0] * grid_cells[1] * grid_cells[2]
    x_first = lax.axis_index(SLAB) * cells_x
    y_first = lax.axis_index("z") * cells_y
    hidden = weight_mid.shape[0]
    rows = cells_x * cells_y * cells_z

    free = (1 - fixed_mask).astype(F32)[None]
    force = free * load_mask.astype(F32)[None] * load_values
    loads = with_planes(with_rows(jnp.concatenate([force, free], 0), 2, 3), 2, 3)

    def centre(first, count, total):
        return ((first + jnp.arange(count, dtype=jnp.int32)).astype(F32) + 0.5) / total

    x_phase = two_pi * (
        centre(x_first, cells_x, grid_cells[0])[:, None, None] * frequencies[0][None, :, None]
        + centre(y_first, cells_y, grid_cells[1])[None, None, :] * frequencies[1][None, :, None]
    )
    z_phase = two_pi * frequencies[2][:, None] * centre(0, cells_z, grid_cells[2])[None, :]
    tables = (jnp.cos(x_phase), jnp.sin(x_phase), jnp.cos(z_phase), jnp.sin(z_phase))
    half = jnp.asarray(0.5, BF)
    out_row = jnp.pad(weight_out[None], ((0, 15), (0, 0)))

    table_specs = [pl.BlockSpec((1,) + x_phase.shape[1:], lambda i: (i, 0, 0))] * 2
    table_specs += [fixed(z_phase.shape)] * 2
    plane_spec = pl.BlockSpec((1, cells_y, cells_z), lambda i: (i, 0, 0))
    plane_shape = jax.ShapeDtypeStruct((cells_x, cells_y, cells_z), F32)
    kept = pltpu.VMEM((hidden, rows), BF)
    density, stiff, hidden_in, slope_mid, slope_in, hidden_mid = pl.pallas_call(
        functools.partial(forward_kernel, width=4),
        name="forward",
        grid=(cells_x,),
        in_specs=table_specs
        + [fixed((hidden, weight_in.shape[0])), fixed((hidden, hidden))]
        + [fixed((hidden, 1)), fixed((16, hidden))],
        out_specs=[plane_spec, plane_spec, WHOLE, WHOLE, WHOLE, WHOLE],
        out_shape=[plane_shape, plane_shape, kept, kept, kept, kept],
        compiler_params=params(20),
    )(
        *tables,
        weight_in.T * half,
        weight_mid.T * half,
        0.5 * weight_out.astype(F32)[:, None],
        out_row,
    )
    stiff = with_planes(with_rows(stiff, 2, 2), 2, 2)

    span = 1024
    back = pl.pallas_call(
        functools.partial(back_kernel, span=span),
        name="back",
        grid=(rows // span,),
        in_specs=[fixed((hidden, hidden)), WHOLE, WHOLE],
        out_specs=WHOLE,
        out_shape=kept,
        input_output_aliases={2: 0},
        compiler_params=params(20),
        cost_estimate=pl.CostEstimate(
            flops=2 * hidden * hidden * rows, bytes_accessed=6 * hidden * rows, transcendentals=0
        ),
    )(weight_mid * half, in_vmem(slope_mid), in_vmem(slope_in))

    devices = lax.axis_size(ALL)
    held = jax.ShapeDtypeStruct((3, cells_x + 1, ROWS, cells_z), F32)
    first, second, sums = pl.pallas_call(
        krylov_kernel,
        name="krylov",
        out_shape=[held, held, jax.ShapeDtypeStruct((devices, 8, 128), F32)],
        compiler_params=params(20),
    )(loads, stiff, density)
    parts = lax.all_to_all(sums, ALL, 0, 0)
    solution, slope = pl.pallas_call(
        functools.partial(energy_kernel, elements_total),
        name="energy",
        out_shape=[jax.ShapeDtypeStruct((3, cells_x, cells_y, cells_z), F32), plane_shape],
        compiler_params=params(20),
    )(parts, loads, first, second, density)

    height = hidden + weight_in.shape[0]
    groups = hidden // 128
    grads, grad_out = pl.pallas_call(
        functools.partial(gradient_kernel, steps=cells_x),
        name="gradients",
        grid=(cells_x,),
        in_specs=[plane_spec] + table_specs + [WHOLE] * 4,
        out_specs=[fixed((groups, height, 128)), fixed((groups, 128))],
        out_shape=[
            jax.ShapeDtypeStruct((groups, height, 128), F32),
            jax.ShapeDtypeStruct((groups, 128), F32),
        ],
        scratch_shapes=[pltpu.VMEM((hidden, 128), F32)],
        compiler_params=params(20),
    )(slope, *tables, *[in_vmem(a) for a in (hidden_in, slope_mid, back, hidden_mid)])
    grads, grad_out = summed_grads(grads, grad_out)
    grads = grads.transpose(1, 0, 2).reshape(height, hidden)
    return (solution, density, grads[hidden:], grads[:hidden], grad_out.reshape(hidden))


def solution(mesh):
    slab, sub = mesh.devices.shape
    fine = Mesh(mesh.devices.reshape(4, 4, slab // 16, sub), ALL)
    field = P(SLAB, "z", None)
    vector = P(None, SLAB, "z", None)
    return jax.shard_map(
        on_device,
        mesh=fine,
        in_specs=(vector, field, field, P(), P(), P(), P()),
        out_specs=(vector, field, P(), P(), P()),
        check_vma=False,
    )
```

profile of v0, /device:TPU:1, one launch (start us, length us, event | category | flops | bytes accessed | tf_op | source)
XLA Modules:
  0.0 172.9 jit_solution(10834400219865068826)
XLA Ops:
  3.2 2.5 %collective-permute-start.1 = (f32[4,4,2,256]{3,2,1,0:T(2,128)S(1)}, f32[4,4,2,256]{3,2,1,0:T(2,128)S(1)}, u32[]{:S(2)}, u32[]{:S(2)}) collective-permute-start(f32[4,4,2,256]{3,2,1,0:T(2,128)S(1)} %pad_maximum_fusion.5), channel_id=1, source_target_pairs={{0,1},{1,2},{2,3},{3,0},{4,5},{5,6},{6,7},{7,4},{8,9},{9,10},{10,1... | collective-permute-start | bytes 98312 | tf_op jit(solution)/shard_map/ppermute | solution.py:379
  11.2 14.0 %forward.1 = (f32[4,8,256]{2,1,0:T(8,128)}, f32[4,8,256]{2,1,0:T(8,128)S(1)}, bf16[512,8192]{1,0:T(8,128)(2,1)S(1)}, bf16[512,8192]{1,0:T(8,128)(2,1)S(1)}, bf16...) custom-call(f32[4,128,8]{2,1,0:T(8,128)S(1)} %get-tuple-element.41.x_cos, ...), custom_call_target="tpu_custom_call" | custom-call | tf_op jit(solution)/shard_map/forward/pallas_call | solution.py:452
  25.2 3.2 %copy-done = bf16[512,8192]{1,0:T(8,128)(2,1)} copy-done((bf16[512,8192]{1,0:T(8,128)(2,1)}, bf16[512,8192]{1,0:T(8,128)(2,1)S(1)}, u32[]{:S(2)}) %copy-start) | copy-done | bytes 8388632
  28.4 3.2 %copy-done.3 = bf16[512,8192]{1,0:T(8,128)(2,1)} copy-done((bf16[512,8192]{1,0:T(8,128)(2,1)}, bf16[512,8192]{1,0:T(8,128)(2,1)S(1)}, u32[]{:S(2)}) %copy-start.3) | copy-done | bytes 8388632
  31.7 3.3 %copy-done.7 = bf16[512,8192]{1,0:T(8,128)(2,1)} copy-done((bf16[512,8192]{1,0:T(8,128)(2,1)}, bf16[512,8192]{1,0:T(8,128)(2,1)S(1)}, u32[]{:S(2)}) %copy-start.7) | copy-done | bytes 8388632
  34.9 3.3 %copy-done.9 = bf16[512,8192]{1,0:T(8,128)(2,1)} copy-done((bf16[512,8192]{1,0:T(8,128)(2,1)}, bf16[512,8192]{1,0:T(8,128)(2,1)S(1)}, u32[]{:S(2)}) %copy-start.9) | copy-done | bytes 8388632
  43.7 2.6 %collective-permute-start.7 = (f32[2,16,256]{2,1,0:T(8,128)S(1)}, f32[2,16,256]{2,1,0:T(8,128)S(1)}, u32[]{:S(2)}, u32[]{:S(2)}) collective-permute-start(f32[2,16,256]{2,1,0:T(8,128)S(1)} %get-tuple-element.43), channel_id=1, source_target_pairs={{0,124},{4,0},{8,4},{12,8},{16,12},{20,16},{24,20},{28,24},{32,28}... | collective-permute-start | bytes 98312 | tf_op jit(solution)/shard_map/ppermute | solution.py:379
  49.8 6.0 %collective-permute-start.3 = (f32[4,3,16,256]{3,2,1,0:T(8,128)S(1)}, f32[4,3,16,256]{3,2,1,0:T(8,128)S(1)}, u32[]{:S(2)}, u32[]{:S(2)}) collective-permute-start(f32[4,3,16,256]{3,2,1,0:T(8,128)S(1)} %slice.71), channel_id=1, source_target_pairs={{0,124},{4,0},{8,4},{12,8},{16,12},{20,16},{24,20},{28,24},{32,28}... | collective-permute-start | bytes 589832 | tf_op jit(solution)/shard_map/ppermute | solution.py:379
  57.0 2.9 %krylov.1 = (f32[3,5,16,256]{3,2,1,0:T(8,128)S(1)}, f32[3,5,16,256]{3,2,1,0:T(8,128)S(1)}, f32[128,8,128]{2,1,0:T(8,128)}) custom-call(f32[4,9,16,256]{3,2,1,0:T(8,128)S(1)} %pad_maximum_fusion.1.loads, f32[8,16,256]{2,1,0:T(8,128)S(1)} %pad_maximum_fusion.3.stiff, f32[4,8,256]{2,1,0:T(8,128)S(1)} %copy-done.11), custom_call_target="tpu_custom_call" | custom-call | tf_op jit(solution)/shard_map/krylov/pallas_call | solution.py:488
  59.9 10.5 %all-to-all-start = ((f32[128,8,128]{2,1,0:T(8,128)}), f32[128,8,128]{2,1,0:T(8,128)S(1)}, u32[]{:S(2)}, u32[]{:S(2)}) async-start(f32[128,8,128]{2,1,0:T(8,128)} %get-tuple-element.20), calls=%async_computation | async-start | bytes 1048576 | tf_op jit(solution)/shard_map/all_to_all | solution.py:494
  70.4 3.4 %copy-done.1 = bf16[512,8192]{1,0:T(8,128)(2,1)S(1)} copy-done((bf16[512,8192]{1,0:T(8,128)(2,1)S(1)}, bf16[512,8192]{1,0:T(8,128)(2,1)}, u32[]{:S(2)}) %copy-start.1) | copy-done | bytes 8388632
  73.8 3.4 %copy-done.4 = bf16[512,8192]{1,0:T(8,128)(2,1)S(1)} copy-done((bf16[512,8192]{1,0:T(8,128)(2,1)S(1)}, bf16[512,8192]{1,0:T(8,128)(2,1)}, u32[]{:S(2)}) %copy-start.4) | copy-done | bytes 8388632
  77.2 5.8 %back.1 = bf16[512,8192]{1,0:T(8,128)(2,1)S(1)} custom-call(bf16[512,512]{1,0:T(8,128)(2,1)S(1)} %get-tuple-element.38.w_mid, bf16[512,8192]{1,0:T(8,128)(2,1)S(1)} %copy-done.1, bf16[512,8192]{1,0:T(8,128)(2,1)S(1)} %copy-done.4), custom_call_target="tpu_custom_call", output_to_operand_aliasing={{}: (2, {})} | custom-call | flops 4294967296 | bytes 25165824 | tf_op jit(solution)/shard_map/back/pallas_call | solution.py:472
  83.0 3.2 %copy-done.5 = bf16[512,8192]{1,0:T(8,128)(2,1)} copy-done((bf16[512,8192]{1,0:T(8,128)(2,1)}, bf16[512,8192]{1,0:T(8,128)(2,1)S(1)}, u32[]{:S(2)}) %copy-start.5) | copy-done | bytes 8388632
  87.1 3.4 %copy-done.2 = bf16[512,8192]{1,0:T(8,128)(2,1)S(1)} copy-done((bf16[512,8192]{1,0:T(8,128)(2,1)S(1)}, bf16[512,8192]{1,0:T(8,128)(2,1)}, u32[]{:S(2)}) %copy-start.2) | copy-done | bytes 8388632
  90.5 3.4 %copy-done.6 = bf16[512,8192]{1,0:T(8,128)(2,1)S(1)} copy-done((bf16[512,8192]{1,0:T(8,128)(2,1)S(1)}, bf16[512,8192]{1,0:T(8,128)(2,1)}, u32[]{:S(2)}) %copy-start.6) | copy-done | bytes 8388632
  93.9 3.4 %copy-done.8 = bf16[512,8192]{1,0:T(8,128)(2,1)S(1)} copy-done((bf16[512,8192]{1,0:T(8,128)(2,1)S(1)}, bf16[512,8192]{1,0:T(8,128)(2,1)}, u32[]{:S(2)}) %copy-start.8) | copy-done | bytes 8388632
  97.3 3.4 %copy-done.10 = bf16[512,8192]{1,0:T(8,128)(2,1)S(1)} copy-done((bf16[512,8192]{1,0:T(8,128)(2,1)S(1)}, bf16[512,8192]{1,0:T(8,128)(2,1)}, u32[]{:S(2)}) %copy-start.10) | copy-done | bytes 8388632
  100.7 13.3 %gradients.1 = (f32[4,768,128]{2,1,0:T(8,128)}, f32[4,128]{1,0:T(4,128)S(1)}) custom-call(f32[4,8,256]{2,1,0:T(8,128)S(1)} %get-tuple-element.24.slope, f32[4,128,8]{2,1,0:T(8,128)S(1)} %get-tuple-element.41.x_cos, f32[4,128,8]{2,1,0:T(8,128)S(1)} %get-tuple-element.40.x_sin, f32[128,256]{1,0:T(8,128)S(1)} %get-tuple-element.50.z_cos, ...), custom_call_target="tpu_custom_call" | custom-call | tf_op jit(solution)/shard_map/gradients/pallas_call | solution.py:504
  116.6 1.9 %collective-permute-done.8 = f32[64,24,128]{2,1,0:T(8,128)S(1)} collective-permute-done((f32[64,24,128]{2,1,0:T(8,128)S(1)}, f32[64,24,128]{2,1,0:T(8,128)S(1)}, u32[]{:S(2)}, u32[]{:S(2)}) %collective-permute-start.8) | collective-permute-done | bytes 786464 | tf_op jit(solution)/shard_map/ppermute | solution.py:409
  118.6 24.1 %all_to_all.15 = f32[64,24,128]{2,1,0:T(8,128)S(1)} all-to-all(f32[64,24,128]{2,1,0:T(8,128)S(1)} %bitcast_add_fusion), channel_id=1, replica_groups=mesh['x'=4,'y'=4,'c'=2,'z'=4] {'x','y','z'}, dimensions={0} | all-to-all | bytes 1572864 | tf_op jit(solution)/shard_map/all_to_all | solution.py:410
  142.9 20.7 %all_to_all.16 = f32[64,28,128]{2,1,0:T(8,128)S(1)} all-to-all(f32[64,28,128]{2,1,0:T(8,128)S(1)} %broadcast_in_dim.56), channel_id=1, replica_groups=mesh['x'=4,'y'=4,'c'=2,'z'=4] {'x','y','z'}, dimensions={0} | all-to-all | bytes 1835008 | tf_op jit(solution)/shard_map/all_to_all | solution.py:412
  163.7 3.5 %collective-permute-start.9 = (f32[64,24,128]{2,1,0:T(8,128)S(1)}, f32[64,24,128]{2,1,0:T(8,128)S(1)}, u32[]{:S(2)}, u32[]{:S(2)}) collective-permute-start(f32[64,24,128]{2,1,0:T(8,128)S(1)} %slice.74), channel_id=1, source_target_pairs={{0,4},{4,0},{1,5},{5,1},{2,6},{6,2},{3,7},{7,3},{8,12},{12,8},{9,1... | collective-permute-start | bytes 2359304 | tf_op jit(solution)/shard_map/ppermute | solution.py:415
  167.4 1.8 %collective-permute-done.10 = f32[4,128]{1,0:T(4,128)S(1)} collective-permute-done((f32[4,128]{1,0:T(4,128)S(1)}, f32[4,128]{1,0:T(4,128)S(1)}, u32[]{:S(2)}, u32[]{:S(2)}) %collective-permute-start.10) | collective-permute-done | bytes 2080 | tf_op jit(solution)/shard_map/ppermute | solution.py:416
  (90 shorter events, 25.8 us)
Async XLA Ops:
  0.6 8.4 %copy-start.13 = (bf16[512,512]{1,0:T(8,128)(2,1)S(1)}, bf16[512,512]{1,0:T(8,128)(2,1)}, u32[]{:S(2)}) copy-start(bf16[512,512]{1,0:T(8,128)(2,1)} %param.12) | copy-start | bytes 1572868
  3.2 44.3 %collective-permute-start.1 = (f32[4,4,2,256]{3,2,1,0:T(2,128)S(1)}, f32[4,4,2,256]{3,2,1,0:T(2,128)S(1)}, u32[]{:S(2)}, u32[]{:S(2)}) collective-permute-start(f32[4,4,2,256]{3,2,1,0:T(2,128)S(1)} %pad_maximum_fusion.5), channel_id=1, source_target_pairs={{0,1},{1,2},{2,3},{3,0},{4,5},{5,6},{6,7},{7,4},{8,9},{9,10},{10,1... | collective-permute-start | bytes 98312 | tf_op jit(solution)/shard_map/ppermute | solution.py:379
  31.7 3.3 %copy-start.7 = (bf16[512,8192]{1,0:T(8,128)(2,1)}, bf16[512,8192]{1,0:T(8,128)(2,1)S(1)}, u32[]{:S(2)}) copy-start(bf16[512,8192]{1,0:T(8,128)(2,1)S(1)} %get-tuple-element.25.hidden_in) | copy-start | bytes 25165828
  34.9 3.3 %copy-start.9 = (bf16[512,8192]{1,0:T(8,128)(2,1)}, bf16[512,8192]{1,0:T(8,128)(2,1)S(1)}, u32[]{:S(2)}) copy-start(bf16[512,8192]{1,0:T(8,128)(2,1)S(1)} %get-tuple-element.28.hidden_mid) | copy-start | bytes 25165828
  38.2 3.7 %collective-permute-start.5 = (f32[4,2,256]{2,1,0:T(2,128)S(1)}, f32[4,2,256]{2,1,0:T(2,128)S(1)}, u32[]{:S(2)}, u32[]{:S(2)}) collective-permute-start(f32[4,2,256]{2,1,0:T(2,128)S(1)} %get-tuple-element.45), channel_id=1, source_target_pairs={{0,1},{1,2},{2,3},{3,0},{4,5},{5,6},{6,7},{7,4},{8,9},{9,10},{10,1... | collective-permute-start | bytes 24584 | tf_op jit(solution)/shard_map/ppermute | solution.py:379
  39.8 9.2 %collective-permute-start = (f32[4,4,3,256]{3,2,1,0:T(4,128)S(1)}, f32[4,4,3,256]{3,2,1,0:T(4,128)S(1)}, u32[]{:S(2)}, u32[]{:S(2)}) collective-permute-start(f32[4,4,3,256]{3,2,1,0:T(4,128)S(1)} %fusion.2), channel_id=1, source_target_pairs={{0,3},{1,0},{2,1},{3,2},{4,7},{5,4},{6,5},{7,6},{8,11},{9,8},{10,9... | collective-permute-start | bytes 147464 | tf_op jit(solution)/shard_map/ppermute | solution.py:379
  40.9 2.7 %collective-permute-start.4 = (f32[4,2,256]{2,1,0:T(2,128)S(1)}, f32[4,2,256]{2,1,0:T(2,128)S(1)}, u32[]{:S(2)}, u32[]{:S(2)}) collective-permute-start(f32[4,2,256]{2,1,0:T(2,128)S(1)} %get-tuple-element.44), channel_id=1, source_target_pairs={{0,3},{1,0},{2,1},{3,2},{4,7},{5,4},{6,5},{7,6},{8,11},{9,8},{10,9... | collective-permute-start | bytes 24584 | tf_op jit(solution)/shard_map/ppermute | solution.py:379
  43.7 5.4 %collective-permute-start.7 = (f32[2,16,256]{2,1,0:T(8,128)S(1)}, f32[2,16,256]{2,1,0:T(8,128)S(1)}, u32[]{:S(2)}, u32[]{:S(2)}) collective-permute-start(f32[2,16,256]{2,1,0:T(8,128)S(1)} %get-tuple-element.43), channel_id=1, source_target_pairs={{0,124},{4,0},{8,4},{12,8},{16,12},{20,16},{24,20},{28,24},{32,28}... | collective-permute-start | bytes 98312 | tf_op jit(solution)/shard_map/ppermute | solution.py:379
  46.2 3.5 %collective-permute-start.6 = (f32[2,16,256]{2,1,0:T(8,128)S(1)}, f32[2,16,256]{2,1,0:T(8,128)S(1)}, u32[]{:S(2)}, u32[]{:S(2)}) collective-permute-start(f32[2,16,256]{2,1,0:T(8,128)S(1)} %get-tuple-element.42), channel_id=1, source_target_pairs={{0,4},{4,8},{8,12},{12,16},{16,20},{20,24},{24,28},{28,32},{32,36}... | collective-permute-start | bytes 98312 | tf_op jit(solution)/shard_map/ppermute | solution.py:379
  49.1 7.9 %copy-start.11 = (f32[4,8,256]{2,1,0:T(8,128)S(1)}, f32[4,8,256]{2,1,0:T(8,128)}, u32[]{:S(2)}) copy-start(f32[4,8,256]{2,1,0:T(8,128)} %get-tuple-element.32.density) | copy-start | bytes 98308
  49.2 6.7 %collective-permute-start.2 = (f32[4,2,16,256]{3,2,1,0:T(8,128)S(1)}, f32[4,2,16,256]{3,2,1,0:T(8,128)S(1)}, u32[]{:S(2)}, u32[]{:S(2)}) collective-permute-start(f32[4,2,16,256]{3,2,1,0:T(8,128)S(1)} %slice.70), channel_id=1, source_target_pairs={{0,4},{4,8},{8,12},{12,16},{16,20},{20,24},{24,28},{28,32},{32,36}... | collective-permute-start | bytes 393224 | tf_op jit(solution)/shard_map/ppermute | solution.py:379
  49.8 7.1 %collective-permute-start.3 = (f32[4,3,16,256]{3,2,1,0:T(8,128)S(1)}, f32[4,3,16,256]{3,2,1,0:T(8,128)S(1)}, u32[]{:S(2)}, u32[]{:S(2)}) collective-permute-start(f32[4,3,16,256]{3,2,1,0:T(8,128)S(1)} %slice.71), channel_id=1, source_target_pairs={{0,124},{4,0},{8,4},{12,8},{16,12},{20,16},{24,20},{28,24},{32,28}... | collective-permute-start | bytes 589832 | tf_op jit(solution)/shard_map/ppermute | solution.py:379
  59.9 26.3 %all-to-all-start = ((f32[128,8,128]{2,1,0:T(8,128)}), f32[128,8,128]{2,1,0:T(8,128)S(1)}, u32[]{:S(2)}, u32[]{:S(2)}) async-start(f32[128,8,128]{2,1,0:T(8,128)} %get-tuple-element.20), calls=%async_computation | async-start | bytes 1048576 | tf_op jit(solution)/shard_map/all_to_all | solution.py:494
  70.4 3.4 %copy-start.1 = (bf16[512,8192]{1,0:T(8,128)(2,1)S(1)}, bf16[512,8192]{1,0:T(8,128)(2,1)}, u32[]{:S(2)}) copy-start(bf16[512,8192]{1,0:T(8,128)(2,1)} %copy-done) | copy-start | bytes 25165828
  73.8 3.4 %copy-start.4 = (bf16[512,8192]{1,0:T(8,128)(2,1)S(1)}, bf16[512,8192]{1,0:T(8,128)(2,1)}, u32[]{:S(2)}) copy-start(bf16[512,8192]{1,0:T(8,128)(2,1)} %copy-done.3) | copy-start | bytes 25165828
  83.0 3.2 %copy-start.5 = (bf16[512,8192]{1,0:T(8,128)(2,1)}, bf16[512,8192]{1,0:T(8,128)(2,1)S(1)}, u32[]{:S(2)}) copy-start(bf16[512,8192]{1,0:T(8,128)(2,1)S(1)} %back.1) | copy-start | bytes 25165828
  87.1 3.4 %copy-start.2 = (bf16[512,8192]{1,0:T(8,128)(2,1)S(1)}, bf16[512,8192]{1,0:T(8,128)(2,1)}, u32[]{:S(2)}) copy-start(bf16[512,8192]{1,0:T(8,128)(2,1)} %copy-done) | copy-start | bytes 25165828
  90.5 3.4 %copy-start.6 = (bf16[512,8192]{1,0:T(8,128)(2,1)S(1)}, bf16[512,8192]{1,0:T(8,128)(2,1)}, u32[]{:S(2)}) copy-start(bf16[512,8192]{1,0:T(8,128)(2,1)} %copy-done.5) | copy-start | bytes 25165828
  93.9 3.4 %copy-start.8 = (bf16[512,8192]{1,0:T(8,128)(2,1)S(1)}, bf16[512,8192]{1,0:T(8,128)(2,1)}, u32[]{:S(2)}) copy-start(bf16[512,8192]{1,0:T(8,128)(2,1)} %copy-done.7) | copy-start | bytes 25165828
  97.3 3.4 %copy-start.10 = (bf16[512,8192]{1,0:T(8,128)(2,1)S(1)}, bf16[512,8192]{1,0:T(8,128)(2,1)}, u32[]{:S(2)}) copy-start(bf16[512,8192]{1,0:T(8,128)(2,1)} %copy-done.9) | copy-start | bytes 25165828
  113.9 4.5 %copy-start.12 = (f32[4,768,128]{2,1,0:T(8,128)S(1)}, f32[4,768,128]{2,1,0:T(8,128)}, u32[]{:S(2)}) copy-start(f32[4,768,128]{2,1,0:T(8,128)} %get-tuple-element.29) | copy-start | bytes 4718596
  115.3 3.2 %collective-permute-start.8 = (f32[64,24,128]{2,1,0:T(8,128)S(1)}, f32[64,24,128]{2,1,0:T(8,128)S(1)}, u32[]{:S(2)}, u32[]{:S(2)}) collective-permute-start(f32[64,24,128]{2,1,0:T(8,128)S(1)} %dynamic-slice_bitcast_fusion), channel_id=1, source_target_pairs={{0,4},{4,0},{1,5},{5,1},{2,6},{6,2},{3,7},{7,3},{8,12},{12,8},{9,1... | collective-permute-start | bytes 2359304 | tf_op jit(solution)/shard_map/ppermute | solution.py:409
  163.7 6.0 %collective-permute-start.9 = (f32[64,24,128]{2,1,0:T(8,128)S(1)}, f32[64,24,128]{2,1,0:T(8,128)S(1)}, u32[]{:S(2)}, u32[]{:S(2)}) collective-permute-start(f32[64,24,128]{2,1,0:T(8,128)S(1)} %slice.74), channel_id=1, source_target_pairs={{0,4},{4,0},{1,5},{5,1},{2,6},{6,2},{3,7},{7,3},{8,12},{12,8},{9,1... | collective-permute-start | bytes 2359304 | tf_op jit(solution)/shard_map/ppermute | solution.py:415
  167.3 1.8 %collective-permute-start.10 = (f32[4,128]{1,0:T(4,128)S(1)}, f32[4,128]{1,0:T(4,128)S(1)}, u32[]{:S(2)}, u32[]{:S(2)}) collective-permute-start(f32[4,128]{1,0:T(4,128)S(1)} %slice_reduce_fusion), channel_id=1, source_target_pairs={{0,4},{4,0},{1,5},{5,1},{2,6},{6,2},{3,7},{7,3},{8,12},{12,8},{9,1... | collective-permute-start | bytes 6152 | tf_op jit(solution)/shard_map/ppermute | solution.py:416
  (2 other events, 6.5 us)
where the time goes:
time: 174 us; the launch traced here: 173 us
  blocking collectives  44.8 us (26%)
  local copies, waits for them, and re-layouts  43.1 us (25%)
  Pallas kernels  36.8 us (21%)
  starting transfers between devices  31.6 us (18%)
  waiting for transfers between devices  8.45 us (5%)
  other arithmetic  7.1 us (4%)
    unnamed x31, local copies, waits for them, and re-layouts  39.9 us
    all_to_all x1, blocking collectives, summed_grads(): share = jnp.sum(lax.all_to_all(half, CHIPS, 0, 0), axis=0)  24.1 us
    all_to_all x1, blocking collectives, summed_grads(): lax.all_to_all(jnp.broadcast_to(share[None], (chips,) + share.shape), CHI...  20.7 us
    ppermute x8, starting transfers between devices, shifted(): got = lax.ppermute(block, axis, route)  16.2 us
    pallas_call x1, Pallas kernels, on_device(): pl.pallas_call(functools.partial(forward_kernel, width=4), name='forward'...  14 us
    pallas_call x1, Pallas kernels, on_device(): pl.pallas_call(functools.partial(gradient_kernel, steps=cells_x), name='g...  13.3 us
    all_to_all x1, starting transfers between devices, on_device(): parts = lax.all_to_all(sums, ALL, 0, 0)  10.5 us
    pallas_call x1, Pallas kernels, on_device(): pl.pallas_call(functools.partial(back_kernel, span=span), name='back', gr...  5.8 us
  transfers between devices with their start and end apart: 12, of which 6 were waited for; matrix products, arithmetic and copies ran while one was open for 4% of the time, Pallas kernels for 11%

commit v1 on v0

v1 whole, which is shorter than its diff:
```python
import functools
import itertools
import math

import jax
import jax.numpy as jnp
import numpy as np
from jax import lax
from jax.experimental import pallas as pl
from jax.experimental.pallas import tpu as pltpu
from jax.sharding import Mesh
from jax.sharding import PartitionSpec as P

ITERS = 3
SLAB = ("x", "y", "c")
CHIPS = ("x", "y", "z")
ALL = ("x", "y", "c", "z")
BF = jnp.bfloat16
F32 = jnp.float32

two_pi = 2.0 * math.pi
emin = 0.001
penalty = 4.0
vol_target = 0.3
ROWS = 16
corner_list = list(itertools.product((0, 1), repeat=3))
LAST = (((1,), (1,)), ((), ()))


def hex_stiffness():
    poisson = 0.3
    lame_first = poisson / ((1.0 + poisson) * (1.0 - 2.0 * poisson))
    lame_second = 0.5 / (1.0 + poisson)
    elastic = np.zeros((6, 6))
    elastic[:3, :3] = lame_first
    for axis_number in range(3):
        elastic[axis_number, axis_number] += 2.0 * lame_second
        elastic[axis_number + 3, axis_number + 3] = lame_second
    gauss_points = [0.5 - 0.5 / math.sqrt(3.0), 0.5 + 0.5 / math.sqrt(3.0)]
    matrix = np.zeros((24, 24))
    for location in itertools.product(gauss_points, repeat=3):
        strain = np.zeros((6, 24))
        for corner_number, corner in enumerate(corner_list):
            factors = [
                location[axis] if corner[axis] == 1 else 1.0 - location[axis] for axis in range(3)
            ]
            slopes = [1.0 if corner[axis] == 1 else -1.0 for axis in range(3)]
            derivative = [
                slopes[0] * factors[1] * factors[2],
                factors[0] * slopes[1] * factors[2],
                factors[0] * factors[1] * slopes[2],
            ]
            column = 3 * corner_number
            for axis in range(3):
                strain[axis, column + axis] = derivative[axis]
            strain[3, column + 1] = derivative[2]
            strain[3, column + 2] = derivative[1]
            strain[4, column + 0] = derivative[2]
            strain[4, column + 2] = derivative[0]
            strain[5, column + 0] = derivative[1]
            strain[5, column + 1] = derivative[0]
        matrix += strain.T @ elastic @ strain / 8.0
    return matrix


def modal_stiffness():
    table = hex_stiffness()
    change = np.zeros((24, 24))
    for row, wave in enumerate(corner_list):
        for column, corner in enumerate(corner_list):
            sign = np.prod([1.0 if c == 1 else -1.0 for w, c in zip(wave, corner) if w == 1])
            for d in range(3):
                change[3 * row + d, 3 * column + d] = sign
    modal = change @ table @ change.T / 64.0
    blocks = []
    for parity in corner_list:
        waves = [tuple(parity[a] ^ (a == d) for a in range(3)) for d in range(3)]
        index = [3 * corner_list.index(wave) + d for d, wave in enumerate(waves)]
        block = modal[np.ix_(index, index)]
        blocks.append((waves, np.where(np.abs(block) < 1e-9, 0.0, block)))
    return blocks


BLOCKS = modal_stiffness()


def lane_mask(shape, lane):
    return lax.broadcasted_iota(jnp.int32, shape, len(shape) - 1) == lane


def plane_modes(plane, rows):
    size = plane.shape[-1]
    ahead = jnp.where(lane_mask(plane.shape, size - 1), 0.0, pltpu.roll(plane, size - 1, 1))
    modes = {}
    for wave_z, part in ((0, plane + ahead), (1, ahead - plane)):
        following = pltpu.roll(part, ROWS - 1, 0)
        modes[0, wave_z] = (part + following)[:rows]
        modes[1, wave_z] = (following - part)[:rows]
    return modes


def element_modes(lower, upper):
    found = []
    for low, high in zip(lower, upper):
        modes = {}
        for key in low:
            modes[(0,) + key] = low[key] + high[key]
            modes[(1,) + key] = high[key] - low[key]
        found.append(modes)
    return found


def modal_forces(modes):
    for waves, block in BLOCKS:
        values = [modes[d][waves[d]] for d in range(3)]
        for d in range(3):
            total = None
            for other in range(3):
                if block[d, other] != 0.0:
                    term = np.float32(block[d, other]) * values[other]
                    total = term if total is None else total + term
            if total is not None:
                yield d, waves[d], values[d], total


def energy_of(modes):
    total = None
    for _, _, value, force in modal_forces(modes):
        total = value * force if total is None else total + value * force
    return total


def node_plane(gathered):
    parts = []
    for wave_z in (0, 1):
        even, odd = gathered[0, wave_z], gathered[1, wave_z]
        parts.append((even - odd) + pltpu.roll(even + odd, 1, 0))
    behind = pltpu.roll(parts[0] + parts[1], 1, 1)
    return (parts[0] - parts[1]) + jnp.where(lane_mask(behind.shape, 0), 0.0, behind)


def operator_planes(planes, stiff, free):
    modes = [[plane_modes(component, ROWS) for component in plane] for plane in planes]
    gathered = [[{} for _ in range(3)] for _ in planes]
    for e in range(len(planes) - 1):
        forces = [{} for _ in range(3)]
        for d, wave, _, force in modal_forces(element_modes(modes[e], modes[e + 1])):
            forces[d][wave] = force * stiff[e]
        for d in range(3):
            for key in itertools.product((0, 1), repeat=2):
                even, odd = forces[d].get((0,) + key), forces[d].get((1,) + key)
                for node, sign in ((e, -1), (e + 1, 1)):
                    if even is None:
                        term = odd if sign == 1 else -odd
                    else:
                        term = even + odd if sign == 1 else even - odd
                    held = gathered[node][d]
                    held[key] = term if key not in held else held[key] + term
    return [
        [node_plane(gathered[n][d]) * free[n - 1] for d in range(3)]
        for n in range(1, len(planes) - 1)
    ]


def kept_if(flag):
    return jnp.where(flag == 0, 1.0, 0.0)


def krylov_kernel(place, loads, loads_behind, loads_ahead, stiff, stiff_behind, stiff_ahead, density,
                  first, second, sums):
    cells = loads.shape[1]
    low, high = kept_if(place[SLAB_FIRST]), kept_if(place[SLAB_LAST])

    def load_planes(d):
        planes = [loads_behind[d, p] * low for p in range(2)]
        planes += [loads[d, p] for p in range(cells)]
        return planes + [loads_ahead[d, p] * high for p in range(3)]

    stiff_planes = [stiff_behind[p] * low for p in range(2)]
    stiff_planes += [stiff[p] for p in range(cells)]
    stiff_planes += [stiff_ahead[p] * high for p in range(2)]
    force = [list(plane) for plane in zip(*[load_planes(d) for d in range(3)])]
    free = load_planes(3)
    image = operator_planes(force, stiff_planes, free[1:-1])
    twice = operator_planes(image, stiff_planes[1:-1], free[2:-2])
    own = (force[2 : 2 + cells], image[1 : 1 + cells], twice[:cells])
    rows = density.shape[1]

    def dot(left, right):
        total = None
        for p in range(cells):
            for d in range(3):
                term = left[p][d][:rows] * right[p][d][:rows]
                total = term if total is None else total + term
        return total

    totals = [dot(own[k // 2], own[(k + 1) // 2]) for k in range(2 * ITERS - 1)]
    modes = [[plane_modes(component, rows) for component in plane] for plane in twice]
    last = None
    volume = None
    for e in range(cells):
        term = stiff_planes[2 + e][:rows] * energy_of(element_modes(modes[e], modes[e + 1]))
        last = term if last is None else last + term
        volume = density[e] if volume is None else volume + density[e]
    totals += [last, volume]
    row_number = lax.broadcasted_iota(jnp.int32, sums.shape, 0)
    result = jnp.zeros(sums.shape, F32)
    for k, total in enumerate(totals):
        scalar = jnp.sum(jnp.sum(total, axis=0, keepdims=True), axis=1, keepdims=True)
        result = jnp.where(row_number == k, scalar, result)
    sums[...] = result
    for p in range(cells + 1):
        for d in range(3):
            first[d, p] = image[1 + p][d]
            second[d, p] = twice[p][d]


def krylov_steps(moments):
    mean = moments[1] / moments[0]
    powers = [None, mean]
    for k in range(2, 2 * ITERS):
        powers.append(powers[-1] * mean)
    scaled = [moments[k] / moments[0] / powers[k] if k else 1.0 for k in range(2 * ITERS)]

    def product(left, right, shift):
        return sum(
            left[i] * right[j] * scaled[i + j + shift]
            for i in range(len(left))
            for j in range(len(right))
        )

    solution = [0.0] * ITERS
    residual = [1.0]
    direction = [1.0]
    norm_now = scaled[0]
    work = 0.0
    for iteration in range(ITERS):
        alpha = norm_now / product(direction, direction, 1)
        work = work + alpha * norm_now
        solution = [
            solution[i] + (alpha * direction[i] if i < len(direction) else 0.0)
            for i in range(ITERS)
        ]
        if iteration + 1 < ITERS:
            image = [0.0] + direction
            residual = [
                (residual[i] if i < len(residual) else 0.0) - alpha * image[i]
                for i in range(len(image))
            ]
            norm_next = product(residual, residual, 0)
            beta = norm_next / norm_now
            direction = [
                residual[i] + (beta * direction[i] if i < len(direction) else 0.0)
                for i in range(len(residual))
            ]
            norm_now = norm_next
    factors = [solution[i] / powers[i + 1] for i in range(ITERS)]
    return factors, work * moments[0] / mean


def energy_kernel(elements, place, sums, loads, loads_ahead, first, second, density, solution, slope):
    rows_of = [sums[k : k + 1, :] for k in range(2 * ITERS + 1)]
    factors, compliance = krylov_steps(rows_of[: 2 * ITERS])
    volume = rows_of[2 * ITERS]
    constant = 2.0 * penalty * (volume / elements - vol_target) / elements
    scale = -3.0 * (1.0 - emin) / compliance
    wide = [jnp.concatenate([value, value], axis=1) for value in factors + [scale, constant]]
    high = kept_if(place[SLAB_LAST])
    cells, rows, _ = density.shape
    modes = []
    for p in range(cells + 1):
        plane = []
        for d in range(3):
            load = loads[d, p] if p < cells else loads_ahead[d, 0] * high
            value = wide[0] * load + wide[1] * first[d, p] + wide[2] * second[d, p]
            if p < cells:
                solution[d, p] = value[:rows]
            plane.append(plane_modes(value, rows))
        modes.append(plane)
    for e in range(cells):
        energy = energy_of(element_modes(modes[e], modes[e + 1]))
        held = density[e]
        slope[e] = (wide[3] * held * held * energy + wide[4]) * held * (1.0 - held)


def column_of(line):
    size = line.shape[1]
    shape = (size, size)
    same = lax.broadcasted_iota(jnp.int32, shape, 0) == lax.broadcasted_iota(jnp.int32, shape, 1)
    return jnp.sum(jnp.where(same, line, 0.0), axis=1, keepdims=True)


def prepare_kernel(
    grid_cells, place, load_values, load_mask, fixed_mask, frequencies, w_in, w_mid, w_out,
    loads, loads_first, loads_last, x_cos, x_sin, z_cos, z_sin, w_in_t, w_mid_t, w_mid_half,
    w_column, w_row,
):
    cells, rows, size = load_mask.shape
    free = (1 - fixed_mask[...]).astype(F32)
    held = free * load_mask[...].astype(F32)
    for d in range(4):
        field = free if d == 3 else held * load_values[d]
        loads[d] = field
        loads_first[d] = field[:, :3]
        loads_last[d] = field[:, rows - 2 :]
    columns = [column_of(frequencies[k : k + 1, :]) for k in range(3)]
    half = rows // 2
    lanes = 2 * cells * half
    number = lax.broadcasted_iota(jnp.int32, (1, lanes), 1)
    side = number // (cells * half)
    plane = (number // half) % cells
    inner = number % half
    row = jnp.where(side == 1, inner + 2, jnp.where(inner < 2, inner, inner + half))
    x_centre = ((place[X_FIRST] + plane).astype(F32) + 0.5) / grid_cells[0]
    y_centre = ((place[Y_FIRST] + row).astype(F32) + 0.5) / grid_cells[1]
    phase = two_pi * (x_centre * columns[0] + y_centre * columns[1])
    cos, sin = jnp.cos(phase), jnp.sin(phase)
    for k in range(2 * cells):
        x_cos[k] = cos[:, k * half : (k + 1) * half]
        x_sin[k] = sin[:, k * half : (k + 1) * half]
    z_number = lax.broadcasted_iota(jnp.int32, (1, size), 1)
    phase = two_pi * (((z_number.astype(F32) + 0.5) / grid_cells[2]) * columns[2])
    z_cos[...] = jnp.cos(phase)
    z_sin[...] = jnp.sin(phase)
    w_in_t[...] = (0.5 * w_in[...].astype(F32)).T.astype(BF)
    middle = 0.5 * w_mid[...].astype(F32)
    w_mid_half[...] = middle.astype(BF)
    w_mid_t[...] = middle.T.astype(BF)
    line = w_out[...].astype(F32)
    w_column[...] = 0.5 * column_of(line)
    w_row[...] = jnp.broadcast_to(line, w_row.shape).astype(BF)


def with_rows(stop, start, block, ahead, behind):
    space = ROWS - block.shape[0] - ahead.shape[0] - behind.shape[0]
    zeros = jnp.zeros((space, block.shape[1]), F32)
    return jnp.concatenate([block, ahead * stop, zeros, behind * start], axis=0)


def load_rows_kernel(place, loads, ahead, behind, joined, to_before, to_next):
    start, stop = kept_if(place[Z_FIRST]), kept_if(place[Z_LAST])
    cells = loads.shape[1]
    for d in range(loads.shape[0]):
        for p in range(cells):
            block = with_rows(stop, start, loads[d, p], ahead[d, p], behind[d, p])
            joined[d, p] = block
            if p < to_before.shape[1]:
                to_before[d, p] = block
            if p >= cells - to_next.shape[1]:
                to_next[d, p - (cells - to_next.shape[1])] = block


def stiff_rows_kernel(place, stiff, ahead, behind, joined, to_before, to_next):
    start, stop = kept_if(place[Z_FIRST]), kept_if(place[Z_LAST])
    cells = stiff.shape[0]
    for p in range(cells):
        block = with_rows(stop, start, stiff[p], ahead[p], behind[p])
        joined[p] = block
        if p < to_before.shape[0]:
            to_before[p] = block
        if p >= cells - to_next.shape[0]:
            to_next[p - (cells - to_next.shape[0])] = block


def gated(half):
    up = 1.0 + jnp.tanh(half)
    value = half * up
    return value, up + value * (2.0 - up)


def features_of(x_cos, x_sin, z_cos, z_sin, column):
    cos = x_cos[0, :, column : column + 1]
    sin = x_sin[0, :, column : column + 1]
    return jnp.concatenate([z_cos * cos - z_sin * sin, z_sin * cos + z_cos * sin], 0).astype(BF)


def forward_columns(tables, weights, kept, spans):
    x_cos, x_sin, z_cos, z_sin = tables
    w_in, w_mid, w_column, w_row = weights
    hidden_in, slope_mid, slope_in, hidden_mid = kept

    def keep(array, value):
        for start, first, count in spans:
            array[:, pl.ds(start, count)] = value[:, first : first + count]

    columns = x_cos.shape[2]
    picked = [features_of(x_cos, x_sin, z_cos[...], z_sin[...], q) for q in range(columns)]
    features = jnp.concatenate(picked, 1)
    value, slope = gated(jnp.dot(w_in[...], features, preferred_element_type=F32))
    value = value.astype(BF)
    keep(hidden_in, value)
    keep(slope_in, slope.astype(BF))
    value, slope = gated(jnp.dot(w_mid[...], value, preferred_element_type=F32))
    value = value.astype(BF)
    keep(hidden_mid, value)
    keep(slope_mid, (w_column[...] * slope).astype(BF))
    logits = jnp.dot(w_row[...], value, preferred_element_type=F32)[:1]
    return 0.5 * jnp.tanh(0.5 * logits) + 0.5


def stiffness_of(density):
    return emin + (1.0 - emin) * (density * density * density)


def outer_kernel(
    x_cos, x_sin, z_cos, z_sin, w_in, w_mid, w_column, w_row,
    density, stiff_first, stiff_last, *kept,
):
    size = density.shape[2]
    start = pl.multiple_of(pl.program_id(0) * (8 * size), 8 * size)
    spans = [(start, 0, 2 * size), (start + 6 * size, 2 * size, 2 * size)]
    tables, weights = (x_cos, x_sin, z_cos, z_sin), (w_in, w_mid, w_column, w_row)
    line = forward_columns(tables, weights, kept, spans)
    for q in range(4):
        part = line[:, q * size : (q + 1) * size]
        density[0, q : q + 1, :] = part
        (stiff_first if q < 2 else stiff_last)[0, q % 2 : q % 2 + 1, :] = stiffness_of(part)


def inner_kernel(
    x_cos, x_sin, z_cos, z_sin, w_in, w_mid, w_column, w_row, outer, *rest,
):
    density, stiff = rest[4:6]
    size = density.shape[2]
    start = pl.multiple_of(pl.program_id(0) * (8 * size), 8 * size)
    tables, weights = (x_cos, x_sin, z_cos, z_sin), (w_in, w_mid, w_column, w_row)
    line = forward_columns(tables, weights, rest[6:], [(start + 2 * size, 0, 4 * size)])
    for r in range(8):
        if 2 <= r < 6:
            part = line[:, (r - 2) * size : (r - 1) * size]
        else:
            q = r if r < 2 else r - 4
            part = outer[0, q : q + 1, :]
        density[0, r : r + 1, :] = part
        stiff[0, r : r + 1, :] = stiffness_of(part)


def back_kernel(w_mid, slope_mid, slope_in, back, *, first, span):
    place = pl.ds(pl.multiple_of(first + pl.program_id(0) * span, span), span)
    product = jnp.dot(w_mid[...], slope_mid[:, place], preferred_element_type=F32)
    back[:, place] = (product * slope_in[:, place].astype(F32)).astype(BF)


def in_three(value):
    high = value.astype(BF)
    rest = value - high.astype(F32)
    middle = rest.astype(BF)
    low = (rest - middle.astype(F32)).astype(BF)
    return jnp.concatenate([high, middle, low, jnp.zeros((13, value.shape[1]), BF)], axis=0)


def gradient_kernel(
    place, slope, x_cos, x_sin, z_cos, z_sin, hidden_in, slope_mid, back, hidden_mid,
    mine, other, grad_out, total, running, *, steps,
):
    step = pl.program_id(0)

    @pl.when(step == 0)
    def _():
        total[...] = jnp.zeros_like(total)
        running[...] = jnp.zeros_like(running)

    rows, size = slope.shape[1:]
    half = rows // 2
    mid = first = out = None
    for number, group in enumerate(((0, 1, 6, 7), (2, 3, 4, 5))):
        lines = [slope[0, r : r + 1, :] for r in group]
        picked = []
        for q in range(half):
            cos, sin = x_cos[number, 0, :, q : q + 1], x_sin[number, 0, :, q : q + 1]
            upper = (z_cos[...] * cos - z_sin[...] * sin) * lines[q]
            lower = (z_sin[...] * cos + z_cos[...] * sin) * lines[q]
            picked.append(jnp.concatenate([upper, lower], 0).astype(BF))
        features = jnp.concatenate(picked, 1)
        line = jnp.concatenate(lines, 1)

        def kept(array):
            pieces, q = [], 0
            while q < half:
                run = 1
                while q + run < half and group[q + run] == group[q] + run:
                    run += 1
                start = pl.multiple_of(step * (rows * size) + group[q] * size, size)
                pieces.append(array[:, pl.ds(start, run * size)])
                q += run
            return pieces[0] if len(pieces) == 1 else jnp.concatenate(pieces, 1)

        hidden = (kept(hidden_in).astype(F32) * line).astype(BF)
        terms = (
            lax.dot_general(hidden, kept(slope_mid), LAST, preferred_element_type=F32),
            lax.dot_general(features, kept(back), LAST, preferred_element_type=F32),
            lax.dot_general(kept(hidden_mid), in_three(line), LAST, preferred_element_type=F32),
        )
        if mid is None:
            mid, first, out = terms
        else:
            mid, first, out = mid + terms[0], first + terms[1], out + terms[2]
    height = mid.shape[0]
    for k in range(total.shape[0]):
        total[k, :height, :] += mid[:, k * 128 : (k + 1) * 128]
        total[k, height:, :] += first[:, k * 128 : (k + 1) * 128]
    running[:, : out.shape[1]] += out

    @pl.when(step == steps - 1)
    def _():
        core = place[CORE]
        for k in range(mine.shape[0]):
            mine[k] = total[2 * core + k]
            other[k] = total[2 * (1 - core) + k]
        line = jnp.sum(running[...].T, axis=0, keepdims=True)
        for k in range(grad_out.shape[0]):
            grad_out[k : k + 1, :] = line[:, k * 128 : (k + 1) * 128]


def finish_kernel(place, half, away, grad_in, grad_mid, grad_out):
    chips = half.shape[0]
    height = half.shape[1] - 2 * grad_out.shape[0]
    middle = grad_mid.shape[0]
    at_first = place[CORE] == 0
    for group in range(4):
        part = pl.ds((group % 2) * (chips // 2), chips // 2)
        own, far = half[part, :height, :], away[part, :height, :]
        picked = jnp.where(at_first, own, far) if group < 2 else jnp.where(at_first, far, own)
        picked = picked.reshape(-1, 128)
        lanes = slice(group * 128, (group + 1) * 128)
        grad_mid[:, lanes] = picked[:middle]
        grad_in[:, lanes] = picked[middle:]
    out = jnp.sum(half[:, height:, :], axis=0) + jnp.sum(away[:, height:, :], axis=0)
    grad_out[...] = out[: grad_out.shape[0]]


VM = pltpu.VMEM
WHOLE = pl.BlockSpec(memory_space=pltpu.VMEM)
SCALARS = pl.BlockSpec(memory_space=pltpu.SMEM)
X_FIRST, Y_FIRST, CORE, SLAB_FIRST, SLAB_LAST, Z_FIRST, Z_LAST = range(7)


def fixed(shape):
    return pl.BlockSpec(shape, lambda i: (0,) * len(shape))


def in_vmem(*arrays):
    return [pltpu.with_memory_space_constraint(array, pltpu.VMEM) for array in arrays]


def params(mebibytes=8):
    return pltpu.CompilerParams(vmem_limit_bytes=mebibytes << 20)


def shaped(*shape, dtype=F32):
    return jax.ShapeDtypeStruct(shape, dtype)


def simple(kernel, name, out_shape, place, *operands):
    return pl.pallas_call(
        kernel,
        name=name,
        in_specs=[SCALARS] + [WHOLE] * len(operands),
        out_specs=[WHOLE] * len(out_shape),
        out_shape=out_shape,
        compiler_params=params(),
    )(place, *operands)


def shifted(block, axis, distance):
    size = lax.axis_size(axis)
    return lax.ppermute(block, axis, [(i, (i + distance) % size) for i in range(size)])


def summed(values):
    values = values + lax.ppermute(values, "c", [(0, 1), (1, 0)])
    for axis in ("z", "y", "x"):
        others = [shifted(values, axis, k) for k in range(1, lax.axis_size(axis))]
        values = values + sum(others)
    return values


def on_device(load_values, load_mask, fixed_mask, frequencies, weight_in, weight_mid, weight_out):
    cells_x, cells_y, cells_z = fixed_mask.shape
    slab, sub = lax.axis_index(SLAB), lax.axis_index("z")
    slabs, subs = lax.axis_size(SLAB), lax.axis_size("z")
    grid_cells = (cells_x * slabs, cells_y * subs, cells_z)
    elements_total = grid_cells[0] * grid_cells[1] * grid_cells[2]
    place = jnp.stack(
        [slab * cells_x, sub * cells_y, lax.axis_index("c")]
        + [(slab == 0) * 1, (slab == slabs - 1) * 1, (sub == 0) * 1, (sub == subs - 1) * 1, slab * 0]
    ).astype(jnp.int32)
    inputs, hidden = weight_in.shape
    rows = cells_x * cells_y * cells_z
    half_rows = cells_y // 2
    field = (cells_x, cells_y, cells_z)
    table = shaped(2 * cells_x, inputs // 2, half_rows)
    (
        loads, loads_first, loads_last, x_cos, x_sin, z_cos, z_sin,
        w_in_t, w_mid_t, w_mid_half, w_column, w_row,
    ) = simple(
        functools.partial(prepare_kernel, grid_cells),
        "prepare",
        [
            shaped(4, *field),
            shaped(4, cells_x, 3, cells_z),
            shaped(4, cells_x, 2, cells_z),
            table,
            table,
            shaped(inputs // 2, cells_z),
            shaped(inputs // 2, cells_z),
            shaped(hidden, inputs, dtype=BF),
            shaped(hidden, hidden, dtype=BF),
            shaped(hidden, hidden, dtype=BF),
            shaped(hidden, 1),
            shaped(16, hidden, dtype=BF),
        ],
        place, load_values, load_mask, fixed_mask, frequencies, weight_in, weight_mid,
        weight_out[None],
    )

    loads_up = shifted(loads_first, "z", -1)
    loads_down = shifted(loads_last, "z", 1)
    weights = (w_in_t, w_mid_t, w_column, w_row)
    weight_specs = [fixed(array.shape) for array in weights]
    x_spec = (1, inputs // 2, half_rows)
    z_specs = [fixed(z_cos.shape)] * 2
    kept = [VM((hidden, rows), BF)] * 4

    def plane_spec(count):
        return pl.BlockSpec((1, count, cells_z), lambda i: (i, 0, 0))

    cost = pl.CostEstimate(
        flops=(inputs + hidden) * hidden * rows,
        bytes_accessed=4 * hidden * rows,
        transcendentals=hidden * rows,
    )
    outer, stiff_first, stiff_last, *stored = pl.pallas_call(
        outer_kernel,
        name="outer",
        grid=(cells_x,),
        in_specs=[pl.BlockSpec(x_spec, lambda i: (i, 0, 0))] * 2 + z_specs + weight_specs,
        out_specs=[plane_spec(half_rows), plane_spec(2), plane_spec(2)] + [WHOLE] * 4,
        out_shape=[
            shaped(cells_x, half_rows, cells_z),
            shaped(cells_x, 2, cells_z),
            shaped(cells_x, 2, cells_z),
        ]
        + kept,
        compiler_params=params(12),
        cost_estimate=cost,
    )(x_cos, x_sin, z_cos, z_sin, *weights)
    loads_16, loads_before, loads_next = simple(
        load_rows_kernel,
        "load_rows",
        [
            shaped(4, cells_x, ROWS, cells_z),
            shaped(4, 3, ROWS, cells_z),
            shaped(4, 2, ROWS, cells_z),
        ],
        place, loads, loads_up, loads_down,
    )
    loads_ahead = shifted(loads_before, SLAB, -1)
    loads_behind = shifted(loads_next, SLAB, 1)
    stiff_up = shifted(stiff_first, "z", -1)
    stiff_down = shifted(stiff_last, "z", 1)
    density, stiff, *stored = pl.pallas_call(
        inner_kernel,
        name="inner",
        grid=(cells_x,),
        in_specs=[pl.BlockSpec(x_spec, lambda i: (cells_x + i, 0, 0))] * 2
        + z_specs
        + weight_specs
        + [plane_spec(half_rows)]
        + [WHOLE] * 4,
        out_specs=[plane_spec(cells_y)] * 2 + [WHOLE] * 4,
        out_shape=[shaped(*field)] * 2 + kept,
        input_output_aliases={9 + k: 2 + k for k in range(4)},
        compiler_params=params(12),
        cost_estimate=cost,
    )(x_cos, x_sin, z_cos, z_sin, *weights, outer, *in_vmem(*stored))
    hidden_in, slope_mid, slope_in, hidden_mid = stored
    stiff_16, stiff_before, stiff_next = simple(
        stiff_rows_kernel,
        "stiff_rows",
        [shaped(cells_x, ROWS, cells_z), shaped(2, ROWS, cells_z), shaped(2, ROWS, cells_z)],
        place, stiff, stiff_up, stiff_down,
    )
    stiff_ahead = shifted(stiff_before, SLAB, -1)
    stiff_behind = shifted(stiff_next, SLAB, 1)

    span = 1024
    back = slope_in
    parts = 2
    for part in range(parts):
        back = pl.pallas_call(
            functools.partial(back_kernel, first=part * (rows // parts), span=span),
            name=f"back_{part}",
            grid=(rows // parts // span,),
            in_specs=[fixed((hidden, hidden)), WHOLE, WHOLE],
            out_specs=WHOLE,
            out_shape=kept[0],
            input_output_aliases={2: 0},
            compiler_params=params(),
            cost_estimate=pl.CostEstimate(
                flops=2 * hidden * hidden * rows // parts,
                bytes_accessed=6 * hidden * rows // parts,
                transcendentals=0,
            ),
        )(w_mid_half, *in_vmem(slope_mid, back))

    held = shaped(3, cells_x + 1, ROWS, cells_z)
    first, second, sums = simple(
        krylov_kernel,
        "krylov",
        [held, held, shaped(8, 128)],
        place, loads_16, loads_behind, loads_ahead, stiff_16, stiff_behind, stiff_ahead, density,
    )
    solution, slope = simple(
        functools.partial(energy_kernel, elements_total),
        "energy",
        [shaped(3, *field), shaped(*field)],
        place, summed(sums), loads_16, loads_ahead, first, second, density,
    )

    height = hidden + inputs
    groups = hidden // 128
    pair = pl.BlockSpec((2, 1) + x_spec[1:], lambda i: (0, i, 0, 0))
    tables = [array.reshape((2, cells_x) + x_spec[1:]) for array in (x_cos, x_sin)]
    mine, other, grad_out = pl.pallas_call(
        functools.partial(gradient_kernel, steps=cells_x),
        name="gradients",
        grid=(cells_x,),
        in_specs=[SCALARS, plane_spec(cells_y), pair, pair] + z_specs + [WHOLE] * 4,
        out_specs=[fixed((groups // 2, height, 128))] * 2 + [fixed((groups, 128))],
        out_shape=[shaped(groups // 2, height, 128)] * 2 + [shaped(groups, 128)],
        scratch_shapes=[VM((groups, height, 128), F32), VM((hidden, 128), F32)],
        compiler_params=params(20),
    )(place, slope, *tables, z_cos, z_sin, *in_vmem(hidden_in, slope_mid, back, hidden_mid))

    chips = lax.axis_size(CHIPS)
    swap = [(0, 1), (1, 0)]
    half = (mine + lax.ppermute(other, "c", swap)).reshape(chips, -1, 128)
    share = jnp.sum(lax.all_to_all(half, CHIPS, 0, 0), axis=0)
    share = jnp.concatenate([share, grad_out, jnp.zeros_like(grad_out)], axis=0)
    half = lax.all_to_all(jnp.broadcast_to(share[None], (chips,) + share.shape), CHIPS, 0, 0)
    away = lax.ppermute(half, "c", swap)
    grad_in, grad_mid, grad_out = simple(
        finish_kernel,
        "finish",
        [shaped(inputs, hidden), shaped(hidden, hidden), shaped(groups, 128)],
        place, half, away,
    )
    return solution, density, grad_in, grad_mid, grad_out.reshape(hidden)


def solution(mesh):
    slab, sub = mesh.devices.shape
    fine = Mesh(mesh.devices.reshape(4, 4, slab // 16, sub), ALL)
    field = P(SLAB, "z", None)
    vector = P(None, SLAB, "z", None)
    return jax.shard_map(
        on_device,
        mesh=fine,
        in_specs=(vector, field, field, P(), P(), P(), P()),
        out_specs=(vector, field, P(), P(), P()),
        check_vma=False,
    )
```

time: 174 us -> 140 us (0.80)
  local copies, waits for them, and re-layouts: 43.1 us -> 6.81 us
  blocking collectives: 44.8 us -> 20.8 us
  waiting for transfers between devices: 8.45 us -> 23.9 us
  starting transfers between devices: 31.6 us -> 42.5 us
  Pallas kernels: 36.8 us -> 41.9 us
  other arithmetic: 7.1 us -> 2.27 us
    unnamed x31 -> x20, local copies, waits for them, and re-layouts: 39.9 us -> 5.85 us
    all_to_all x2 -> x1, blocking collectives: 44.8 us -> 20.8 us  [on_device(): lax.all_to_all(jnp.broadcast_to(share[None], (chips,) + share.shape), CHI...]
    ppermute x11 -> x20, starting transfers between devices: 21.1 us -> 36.9 us  [the longest x17 23.9 us: shifted(): lax.ppermute(block, axis, [(i, (i + distance) % size) for i in range(size)])]
    all_to_all x1, waiting for transfers between devices: 0.01 us -> 14.5 us  [on_device(): share = jnp.sum(lax.all_to_all(half, CHIPS, 0, 0), axis=0)]
    pallas_call x4 -> x10, Pallas kernels: 23.6 us -> 29.7 us  [the longest x6 8.86 us: simple(): pl.pallas_call(kernel, name=name, in_specs=[SCALARS] + [WHOLE] * len(oper...]
    all_to_all x1, starting transfers between devices: 10.5 us -> 5.62 us  [on_device(): share = jnp.sum(lax.all_to_all(half, CHIPS, 0, 0), axis=0)]
    mul x8 -> x0, other arithmetic: 3.41 us -> none  [the longest x2 1.68 us: on_device(): force = free * load_mask.astype(F32)[None] * load_values]
    add x1 -> x5, other arithmetic: 0.08 us -> 2.11 us  [the longest x1 2.09 us: on_device(): half = (mine + lax.ppermute(other, 'c', swap)).reshape(chips, -1, 128)]
  transfers between devices with their start and end apart: 12 -> 21, of which waited for: 6 -> 9; matrix products, arithmetic and copies ran while one was open for 4% -> 0% of each run, Pallas kernels for 11% -> 16%
where the time goes in v1:
time: 140 us; the launch traced here: 139 us
  starting transfers between devices  42.5 us (30%)
  Pallas kernels  41.9 us (30%)
  waiting for transfers between devices  23.9 us (17%)
  blocking collectives  20.8 us (15%)
  local copies, waits for them, and re-layouts  6.81 us (5%)
  other arithmetic  2.27 us (2%)
    ppermute x17, starting transfers between devices, shifted(): lax.ppermute(block, axis, [(i, (i + distance) % size) for i in range(size)])  23.9 us
    all_to_all x1, blocking collectives, on_device(): lax.all_to_all(jnp.broadcast_to(share[None], (chips,) + share.shape), CHI...  20.8 us
    all_to_all x1, waiting for transfers between devices, on_device(): share = jnp.sum(lax.all_to_all(half, CHIPS, 0, 0), axis=0)  14.5 us
    pallas_call x1, Pallas kernels, on_device(): pl.pallas_call(functools.partial(gradient_kernel, steps=cells_x), name='g...  12.1 us
    pallas_call x6, Pallas kernels, simple(): pl.pallas_call(kernel, name=name, in_specs=[SCALARS] + [WHOLE] * len(oper...  8.86 us
    pallas_call x1, Pallas kernels, on_device(): pl.pallas_call(inner_kernel, name='inner', grid=(cells_x,), in_specs=[pl....  7.8 us
    pallas_call x1, Pallas kernels, on_device(): pl.pallas_call(outer_kernel, name='outer', grid=(cells_x,), in_specs=[pl....  7.2 us
    pallas_call x2, Pallas kernels, on_device(): pl.pallas_call(functools.partial(back_kernel, first=part * (rows // parts...  5.88 us
  transfers between devices with their start and end apart: 21, of which 9 were waited for; matrix products, arithmetic and copies ran while one was open for 0% of the time, Pallas kernels for 16%

profile of v1, /device:TPU:1, one launch (start us, length us, event | category | flops | bytes accessed | tf_op | source)
XLA Modules:
  0.0 139.0 jit_solution(12247074625110987361)
XLA Ops:
  6.5 1.9 %prepare.1 = (f32[4,4,8,256]{3,2,1,0:T(8,128)S(1)}, f32[4,4,3,256]{3,2,1,0:T(4,128)S(1)}, f32[4,4,2,256]{3,2,1,0:T(2,128)S(1)}, f32[8,128,4]{2,1,0:T(8,128)S(1)}...) custom-call(s32[8]{0:T(128)S(1)} %stack.47.place, ...), custom_call_target="tpu_custom_call" | custom-call | tf_op jit(solution)/shard_map/prepare/pallas_call | solution.py:555
  8.5 4.7 %collective-permute-start = (f32[4,4,3,256]{3,2,1,0:T(4,128)S(1)}, f32[4,4,3,256]{3,2,1,0:T(4,128)S(1)}, u32[]{:S(2)}, u32[]{:S(2)}) collective-permute-start(f32[4,4,3,256]{3,2,1,0:T(4,128)S(1)} %get-tuple-element.48), channel_id=1, source_target_pairs={{0,3},{1,0},{2,1},{3,2},{4,7},{5,4},{6,5},{7,6},{8,11},{9,8},{10,9... | collective-permute-start | bytes 147464 | tf_op jit(solution)/shard_map/ppermute | solution.py:567
  13.1 7.2 %outer.1 = (f32[4,4,256]{2,1,0:T(4,128)S(1)}, f32[4,2,256]{2,1,0:T(2,128)S(1)}, f32[4,2,256]{2,1,0:T(2,128)S(1)}, bf16[512,8192]{1,0:T(8,128)(2,1)S(1)}, bf16[51...) custom-call(f32[8,128,4]{2,1,0:T(8,128)S(1)} %get-tuple-element.53.x_cos, ...), custom_call_target="tpu_custom_call" | custom-call | flops 3221225472 | bytes 16777216 | tf_op jit(solution)/shard_map/outer/pallas_call | solution.py:633
  20.3 2.7 %collective-permute-start.4 = (f32[4,2,256]{2,1,0:T(2,128)S(1)}, f32[4,2,256]{2,1,0:T(2,128)S(1)}, u32[]{:S(2)}, u32[]{:S(2)}) collective-permute-start(f32[4,2,256]{2,1,0:T(2,128)S(1)} %get-tuple-element.67), channel_id=1, source_target_pairs={{0,3},{1,0},{2,1},{3,2},{4,7},{5,4},{6,5},{7,6},{8,11},{9,8},{10,9... | collective-permute-start | bytes 24584 | tf_op jit(solution)/shard_map/ppermute | solution.py:567
  23.7 1.6 %collective-permute-start.3 = (f32[4,3,16,256]{3,2,1,0:T(8,128)S(1)}, f32[4,3,16,256]{3,2,1,0:T(8,128)S(1)}, u32[]{:S(2)}, u32[]{:S(2)}) collective-permute-start(f32[4,3,16,256]{3,2,1,0:T(8,128)S(1)} %get-tuple-element.52), channel_id=1, source_target_pairs={{0,124},{4,0},{8,4},{12,8},{16,12},{20,16},{24,20},{28,24},{32,28}... | collective-permute-start | bytes 589832 | tf_op jit(solution)/shard_map/ppermute | solution.py:567
  26.5 7.8 %inner.1 = (f32[4,8,256]{2,1,0:T(8,128)}, f32[4,8,256]{2,1,0:T(8,128)S(1)}, bf16[512,8192]{1,0:T(8,128)(2,1)S(1)}, bf16[512,8192]{1,0:T(8,128)(2,1)S(1)}, bf16[5...) custom-call(f32[8,128,4]{2,1,0:T(8,128)S(1)} %get-tuple-element.53.x, ...), custom_call_target="tpu_custom_call", output_to_operand_aliasing={{2}: (9, {}), {3}: (10, {}), {4}: (11, {}), {5}: (12, {})} | custom-call | flops 3221225472 | bytes 16777216 | tf_op jit(solution)/shard_map/inner/pallas_call | solution.py:662
  35.4 2.2 %collective-permute-start.7 = (f32[2,16,256]{2,1,0:T(8,128)S(1)}, f32[2,16,256]{2,1,0:T(8,128)S(1)}, u32[]{:S(2)}, u32[]{:S(2)}) collective-permute-start(f32[2,16,256]{2,1,0:T(8,128)S(1)} %get-tuple-element.71), channel_id=1, source_target_pairs={{0,124},{4,0},{8,4},{12,8},{16,12},{20,16},{24,20},{28,24},{32,28}... | collective-permute-start | bytes 98312 | tf_op jit(solution)/shard_map/ppermute | solution.py:567
  39.5 2.6 %krylov.1 = (f32[3,5,16,256]{3,2,1,0:T(8,128)S(1)}, f32[3,5,16,256]{3,2,1,0:T(8,128)S(1)}, f32[8,128]{1,0:T(8,128)S(1)}) custom-call(s32[8]{0:T(128)S(1)} %stack.47.place, f32[4,4,16,256]{3,2,1,0:T(8,128)S(1)} %get-tuple-element.50.loads, f32[4,2,16,256]{3,2,1,0:T(8,128)S(1)} %collective-permute-done.2.loads_behind, ...), custom_call_target="tpu_custom_call" | custom-call | tf_op jit(solution)/shard_map/krylov/pallas_call | solution.py:555
  42.1 5.5 %collective-permute-start.8 = (f32[8,128]{1,0:T(8,128)S(1)}, f32[8,128]{1,0:T(8,128)S(1)}, u32[]{:S(2)}, u32[]{:S(2)}) collective-permute-start(f32[8,128]{1,0:T(8,128)S(1)} %get-tuple-element.73), channel_id=1, source_target_pairs={{0,4},{4,0},{1,5},{5,1},{2,6},{6,2},{3,7},{7,3},{8,12},{12,8},{9,1... | collective-permute-start | bytes 12296 | tf_op jit(solution)/shard_map/ppermute | solution.py:571
  53.1 1.8 %collective-permute-done.9 = f32[8,128]{1,0:T(8,128)S(1)} collective-permute-done((f32[8,128]{1,0:T(8,128)S(1)}, f32[8,128]{1,0:T(8,128)S(1)}, u32[]{:S(2)}, u32[]{:S(2)}) %collective-permute-start.9) | collective-permute-done | bytes 4128 | tf_op jit(solution)/shard_map/ppermute | solution.py:567
  54.9 1.6 %collective-permute-start.13 = (f32[8,128]{1,0:T(8,128)S(1)}, f32[8,128]{1,0:T(8,128)S(1)}, u32[]{:S(2)}, u32[]{:S(2)}) collective-permute-start(f32[8,128]{1,0:T(8,128)S(1)} %add_add_fusion.2), channel_id=1, source_target_pairs={{0,16},{8,24},{16,0},{24,8},{1,17},{9,25},{17,1},{25,9},{2,18},{10... | collective-permute-start | bytes 12296 | tf_op jit(solution)/shard_map/ppermute | solution.py:567
  57.5 2.9 %back_0.1.slope_in = bf16[512,8192]{1,0:T(8,128)(2,1)S(1)} custom-call(bf16[512,512]{1,0:T(8,128)(2,1)S(1)} %get-tuple-element.80.w_mid, bf16[512,8192]{1,0:T(8,128)(2,1)S(1)} %get-tuple-element.79.slope_mid, bf16[512,8192]{1,0:T(8,128)(2,1)S(1)} %get-tuple-element.81.slope_in), custom_call_target="tpu_custom_call", output_to_operand_aliasing={{}: (2, {})} | custom-call | flops 2147483648 | bytes 12582912 | tf_op jit(solution)/shard_map/back_0/pallas_call | solution.py:691
  60.7 4.9 %collective-permute-start.16 = (f32[8,128]{1,0:T(8,128)S(1)}, f32[8,128]{1,0:T(8,128)S(1)}, u32[]{:S(2)}, u32[]{:S(2)}) collective-permute-start(f32[8,128]{1,0:T(8,128)S(1)} %add_add_fusion.1), channel_id=1, source_target_pairs={{0,64},{32,96},{64,0},{96,32},{1,65},{33,97},{65,1},{97,33},{2,66}... | collective-permute-start | bytes 12296 | tf_op jit(solution)/shard_map/ppermute | solution.py:567
  65.6 2.9 %back_1.1.back = bf16[512,8192]{1,0:T(8,128)(2,1)S(1)} custom-call(bf16[512,512]{1,0:T(8,128)(2,1)S(1)} %get-tuple-element.80.w_mid, bf16[512,8192]{1,0:T(8,128)(2,1)S(1)} %get-tuple-element.79.slope_mid, bf16[512,8192]{1,0:T(8,128)(2,1)S(1)} %back_0.1.slope_in), custom_call_target="tpu_custom_call", output_to_operand_aliasing={{}: (2, {})} | custom-call | flops 2147483648 | bytes 12582912 | tf_op jit(solution)/shard_map/back_1/pallas_call | solution.py:691
  69.9 12.1 %gradients.1 = (f32[2,768,128]{2,1,0:T(8,128)}, f32[2,768,128]{2,1,0:T(8,128)}, f32[4,128]{1,0:T(4,128)S(1)}) custom-call(s32[8]{0:T(128)S(1)} %stack.47.place, f32[4,8,256]{2,1,0:T(8,128)S(1)} %get-tuple-element.77.slope, f32[2,4,128,4]{3,2,1,0:T(8,128)S(1)} %bitcast.13, f32[2,4,128,4]{3,2,1,0:T(8,128)S(1)} %bitcast.14, ...), custom_call_target="tpu_custom_call" | custom-call | tf_op jit(solution)/shard_map/gradients/pallas_call | solution.py:725
  82.0 3.9 %collective-permute-start.18 = (f32[2,768,128]{2,1,0:T(8,128)}, f32[2,768,128]{2,1,0:T(8,128)S(1)}, u32[]{:S(2)}, u32[]{:S(2)}) collective-permute-start(f32[2,768,128]{2,1,0:T(8,128)} %get-tuple-element.84), channel_id=1, source_target_pairs={{0,4},{4,0},{1,5},{5,1},{2,6},{6,2},{3,7},{7,3},{8,12},{12,8},{9,1... | collective-permute-start | bytes 2359304 | tf_op jit(solution)/shard_map/ppermute | solution.py:738
  86.0 2.1 %collective-permute-done.18 = f32[2,768,128]{2,1,0:T(8,128)S(1)} collective-permute-done((f32[2,768,128]{2,1,0:T(8,128)}, f32[2,768,128]{2,1,0:T(8,128)S(1)}, u32[]{:S(2)}, u32[]{:S(2)}) %collective-permute-start.18) | collective-permute-done | bytes 786464 | tf_op jit(solution)/shard_map/ppermute | solution.py:738
  88.1 2.1 %add.51 = f32[2,768,128]{2,1,0:T(8,128)} add(f32[2,768,128]{2,1,0:T(8,128)} %get-tuple-element.83, f32[2,768,128]{2,1,0:T(8,128)S(1)} %collective-permute-done.18) | non-fusion elementwise | flops 196608 | bytes 2359296 | tf_op jit(solution)/shard_map/add | solution.py:738
  90.2 5.6 %all-to-all-start = ((f32[64,24,128]{2,1,0:T(8,128)}), f32[64,24,128]{2,1,0:T(8,128)S(1)}, u32[]{:S(2)}, u32[]{:S(2)}) async-start(f32[64,24,128]{2,1,0:T(8,128)} %bitcast.9), calls=%async_computation | async-start | bytes 1572864 | tf_op jit(solution)/shard_map/all_to_all | solution.py:739
  95.9 14.5 %all-to-all-done = f32[64,24,128]{2,1,0:T(8,128)S(1)} async-done(((f32[64,24,128]{2,1,0:T(8,128)}), f32[64,24,128]{2,1,0:T(8,128)S(1)}, u32[]{:S(2)}, u32[]{:S(2)}) %all-to-all-start) | async-done | bytes 786464 | tf_op jit(solution)/shard_map/all_to_all | solution.py:739
  110.6 20.8 %all_to_all.10.half = f32[64,32,128]{2,1,0:T(8,128)S(1)} all-to-all(f32[64,32,128]{2,1,0:T(8,128)S(1)} %broadcast_in_dim.14), channel_id=1, replica_groups=mesh['x'=4,'y'=4,'c'=2,'z'=4] {'x','y','z'}, dimensions={0} | all-to-all | bytes 2097152 | tf_op jit(solution)/shard_map/all_to_all | solution.py:741
  131.4 3.5 %collective-permute-start.19 = (f32[64,32,128]{2,1,0:T(8,128)S(1)}, f32[64,32,128]{2,1,0:T(8,128)S(1)}, u32[]{:S(2)}, u32[]{:S(2)}) collective-permute-start(f32[64,32,128]{2,1,0:T(8,128)S(1)} %all_to_all.10.half), channel_id=1, source_target_pairs={{0,4},{4,0},{1,5},{5,1},{2,6},{6,2},{3,7},{7,3},{8,12},{12,8},{9,1... | collective-permute-start | bytes 3145736 | tf_op jit(solution)/shard_map/ppermute | solution.py:742
  134.9 2.3 %collective-permute-done.19.away = f32[64,32,128]{2,1,0:T(8,128)S(1)} collective-permute-done((f32[64,32,128]{2,1,0:T(8,128)S(1)}, f32[64,32,128]{2,1,0:T(8,128)S(1)}, u32[]{:S(2)}, u32[]{:S(2)}) %collective-permute-start.19) | collective-permute-done | bytes 1048608 | tf_op jit(solution)/shard_map/ppermute | solution.py:742
  137.1 1.8 %finish.1 = (f32[256,512]{1,0:T(8,128)}, f32[512,512]{1,0:T(8,128)}, f32[4,128]{1,0:T(4,128)}) custom-call(s32[8]{0:T(128)S(1)} %stack.47.place, f32[64,32,128]{2,1,0:T(8,128)S(1)} %all_to_all.10.half, f32[64,32,128]{2,1,0:T(8,128)S(1)} %collective-permute-done.19.away), custom_call_target="tpu_custom_call" | custom-call | tf_op jit(solution)/shard_map/finish/pallas_call | solution.py:555
  (63 shorter events, 19.1 us)
Async XLA Ops:
  8.5 14.6 %collective-permute-start = (f32[4,4,3,256]{3,2,1,0:T(4,128)S(1)}, f32[4,4,3,256]{3,2,1,0:T(4,128)S(1)}, u32[]{:S(2)}, u32[]{:S(2)}) collective-permute-start(f32[4,4,3,256]{3,2,1,0:T(4,128)S(1)} %get-tuple-element.48), channel_id=1, source_target_pairs={{0,3},{1,0},{2,1},{3,2},{4,7},{5,4},{6,5},{7,6},{8,11},{9,8},{10,9... | collective-permute-start | bytes 147464 | tf_op jit(solution)/shard_map/ppermute | solution.py:567
  13.1 10.0 %collective-permute-start.1 = (f32[4,4,2,256]{3,2,1,0:T(2,128)S(1)}, f32[4,4,2,256]{3,2,1,0:T(2,128)S(1)}, u32[]{:S(2)}, u32[]{:S(2)}) collective-permute-start(f32[4,4,2,256]{3,2,1,0:T(2,128)S(1)} %get-tuple-element.49), channel_id=1, source_target_pairs={{0,1},{1,2},{2,3},{3,0},{4,5},{5,6},{6,7},{7,4},{8,9},{9,10},{10,1... | collective-permute-start | bytes 98312 | tf_op jit(solution)/shard_map/ppermute | solution.py:567
  20.3 14.0 %collective-permute-start.4 = (f32[4,2,256]{2,1,0:T(2,128)S(1)}, f32[4,2,256]{2,1,0:T(2,128)S(1)}, u32[]{:S(2)}, u32[]{:S(2)}) collective-permute-start(f32[4,2,256]{2,1,0:T(2,128)S(1)} %get-tuple-element.67), channel_id=1, source_target_pairs={{0,3},{1,0},{2,1},{3,2},{4,7},{5,4},{6,5},{7,6},{8,11},{9,8},{10,9... | collective-permute-start | bytes 24584 | tf_op jit(solution)/shard_map/ppermute | solution.py:567
  23.1 11.2 %collective-permute-start.5 = (f32[4,2,256]{2,1,0:T(2,128)S(1)}, f32[4,2,256]{2,1,0:T(2,128)S(1)}, u32[]{:S(2)}, u32[]{:S(2)}) collective-permute-start(f32[4,2,256]{2,1,0:T(2,128)S(1)} %get-tuple-element.68), channel_id=1, source_target_pairs={{0,1},{1,2},{2,3},{3,0},{4,5},{5,6},{6,7},{7,4},{8,9},{9,10},{10,1... | collective-permute-start | bytes 24584 | tf_op jit(solution)/shard_map/ppermute | solution.py:567
  23.7 15.1 %collective-permute-start.3 = (f32[4,3,16,256]{3,2,1,0:T(8,128)S(1)}, f32[4,3,16,256]{3,2,1,0:T(8,128)S(1)}, u32[]{:S(2)}, u32[]{:S(2)}) collective-permute-start(f32[4,3,16,256]{3,2,1,0:T(8,128)S(1)} %get-tuple-element.52), channel_id=1, source_target_pairs={{0,124},{4,0},{8,4},{12,8},{16,12},{20,16},{24,20},{28,24},{32,28}... | collective-permute-start | bytes 589832 | tf_op jit(solution)/shard_map/ppermute | solution.py:567
  25.3 13.5 %collective-permute-start.2 = (f32[4,2,16,256]{3,2,1,0:T(8,128)S(1)}, f32[4,2,16,256]{3,2,1,0:T(8,128)S(1)}, u32[]{:S(2)}, u32[]{:S(2)}) collective-permute-start(f32[4,2,16,256]{3,2,1,0:T(8,128)S(1)} %get-tuple-element.51), channel_id=1, source_target_pairs={{0,4},{4,8},{8,12},{12,16},{16,20},{20,24},{24,28},{28,32},{32,36}... | collective-permute-start | bytes 393224 | tf_op jit(solution)/shard_map/ppermute | solution.py:567
  34.3 26.2 %copy-start = (bf16[512,8192]{1,0:T(8,128)(2,1)}, bf16[512,8192]{1,0:T(8,128)(2,1)S(1)}, u32[]{:S(2)}) copy-start(bf16[512,8192]{1,0:T(8,128)(2,1)S(1)} %get-tuple-element.78.hidden_in) | copy-start | bytes 25165828
  34.9 3.3 %collective-permute-start.6 = (f32[2,16,256]{2,1,0:T(8,128)S(1)}, f32[2,16,256]{2,1,0:T(8,128)S(1)}, u32[]{:S(2)}, u32[]{:S(2)}) collective-permute-start(f32[2,16,256]{2,1,0:T(8,128)S(1)} %get-tuple-element.70), channel_id=1, source_target_pairs={{0,4},{4,8},{8,12},{12,16},{16,20},{20,24},{24,28},{28,32},{32,36}... | collective-permute-start | bytes 98312 | tf_op jit(solution)/shard_map/ppermute | solution.py:567
  35.4 3.3 %collective-permute-start.7 = (f32[2,16,256]{2,1,0:T(8,128)S(1)}, f32[2,16,256]{2,1,0:T(8,128)S(1)}, u32[]{:S(2)}, u32[]{:S(2)}) collective-permute-start(f32[2,16,256]{2,1,0:T(8,128)S(1)} %get-tuple-element.71), channel_id=1, source_target_pairs={{0,124},{4,0},{8,4},{12,8},{16,12},{20,16},{24,20},{28,24},{32,28}... | collective-permute-start | bytes 98312 | tf_op jit(solution)/shard_map/ppermute | solution.py:567
  42.1 6.4 %collective-permute-start.8 = (f32[8,128]{1,0:T(8,128)S(1)}, f32[8,128]{1,0:T(8,128)S(1)}, u32[]{:S(2)}, u32[]{:S(2)}) collective-permute-start(f32[8,128]{1,0:T(8,128)S(1)} %get-tuple-element.73), channel_id=1, source_target_pairs={{0,4},{4,0},{1,5},{5,1},{2,6},{6,2},{3,7},{7,3},{8,12},{12,8},{9,1... | collective-permute-start | bytes 12296 | tf_op jit(solution)/shard_map/ppermute | solution.py:571
  48.5 4.0 %collective-permute-start.10 = (f32[8,128]{1,0:T(8,128)S(1)}, f32[8,128]{1,0:T(8,128)S(1)}, u32[]{:S(2)}, u32[]{:S(2)}) collective-permute-start(f32[8,128]{1,0:T(8,128)S(1)} %add.41), channel_id=1, source_target_pairs={{0,2},{1,3},{2,0},{3,1},{4,6},{5,7},{6,4},{7,5},{8,10},{9,11},{10,... | collective-permute-start | bytes 12296 | tf_op jit(solution)/shard_map/ppermute | solution.py:567
  49.8 3.3 %collective-permute-start.11 = (f32[8,128]{1,0:T(8,128)S(1)}, f32[8,128]{1,0:T(8,128)S(1)}, u32[]{:S(2)}, u32[]{:S(2)}) collective-permute-start(f32[8,128]{1,0:T(8,128)S(1)} %add.41), channel_id=1, source_target_pairs={{0,3},{1,0},{2,1},{3,2},{4,7},{5,4},{6,5},{7,6},{8,11},{9,8},{10,9... | collective-permute-start | bytes 12296 | tf_op jit(solution)/shard_map/ppermute | solution.py:567
  51.2 3.7 %collective-permute-start.9 = (f32[8,128]{1,0:T(8,128)S(1)}, f32[8,128]{1,0:T(8,128)S(1)}, u32[]{:S(2)}, u32[]{:S(2)}) collective-permute-start(f32[8,128]{1,0:T(8,128)S(1)} %add.41), channel_id=1, source_target_pairs={{0,1},{1,2},{2,3},{3,0},{4,5},{5,6},{6,7},{7,4},{8,9},{9,10},{10,1... | collective-permute-start | bytes 12296 | tf_op jit(solution)/shard_map/ppermute | solution.py:567
  54.8 5.6 %collective-permute-start.12 = (f32[8,128]{1,0:T(8,128)S(1)}, f32[8,128]{1,0:T(8,128)S(1)}, u32[]{:S(2)}, u32[]{:S(2)}) collective-permute-start(f32[8,128]{1,0:T(8,128)S(1)} %add_add_fusion.2), channel_id=1, source_target_pairs={{0,8},{8,16},{16,24},{24,0},{1,9},{9,17},{17,25},{25,1},{2,10},{10... | collective-permute-start | bytes 12296 | tf_op jit(solution)/shard_map/ppermute | solution.py:567
  54.9 5.6 %collective-permute-start.13 = (f32[8,128]{1,0:T(8,128)S(1)}, f32[8,128]{1,0:T(8,128)S(1)}, u32[]{:S(2)}, u32[]{:S(2)}) collective-permute-start(f32[8,128]{1,0:T(8,128)S(1)} %add_add_fusion.2), channel_id=1, source_target_pairs={{0,16},{8,24},{16,0},{24,8},{1,17},{9,25},{17,1},{25,9},{2,18},{10... | collective-permute-start | bytes 12296 | tf_op jit(solution)/shard_map/ppermute | solution.py:567
  56.4 4.1 %collective-permute-start.14 = (f32[8,128]{1,0:T(8,128)S(1)}, f32[8,128]{1,0:T(8,128)S(1)}, u32[]{:S(2)}, u32[]{:S(2)}) collective-permute-start(f32[8,128]{1,0:T(8,128)S(1)} %add_add_fusion.2), channel_id=1, source_target_pairs={{0,24},{8,0},{16,8},{24,16},{1,25},{9,1},{17,9},{25,17},{2,26},{10... | collective-permute-start | bytes 12296 | tf_op jit(solution)/shard_map/ppermute | solution.py:567
  60.5 9.4 %slice-start = ((s8[8388608]{0:T(1024)(128)(4,1)}), s8[4194304]{0:T(1024)(128)(4,1)S(1)}, s32[]{:S(2)}) async-start(s8[8388608]{0:T(1024)(128)(4,1)} %bitcast.11), calls=%async_computation.2 | async-start | bytes 8388608
  60.5 9.4 %slice-start.1 = ((s8[8388608]{0:T(1024)(128)(4,1)}), s8[4194304]{0:T(1024)(128)(4,1)S(1)}, s32[]{:S(2)}) async-start(s8[8388608]{0:T(1024)(128)(4,1)} %bitcast.11), calls=%async_computation.3 | async-start | bytes 8388608
  60.6 8.0 %collective-permute-start.15 = (f32[8,128]{1,0:T(8,128)S(1)}, f32[8,128]{1,0:T(8,128)S(1)}, u32[]{:S(2)}, u32[]{:S(2)}) collective-permute-start(f32[8,128]{1,0:T(8,128)S(1)} %add_add_fusion.1), channel_id=1, source_target_pairs={{0,32},{32,64},{64,96},{96,0},{1,33},{33,65},{65,97},{97,1},{2,34}... | collective-permute-start | bytes 12296 | tf_op jit(solution)/shard_map/ppermute | solution.py:567
  60.7 7.8 %collective-permute-start.16 = (f32[8,128]{1,0:T(8,128)S(1)}, f32[8,128]{1,0:T(8,128)S(1)}, u32[]{:S(2)}, u32[]{:S(2)}) collective-permute-start(f32[8,128]{1,0:T(8,128)S(1)} %add_add_fusion.1), channel_id=1, source_target_pairs={{0,64},{32,96},{64,0},{96,32},{1,65},{33,97},{65,1},{97,33},{2,66}... | collective-permute-start | bytes 12296 | tf_op jit(solution)/shard_map/ppermute | solution.py:567
  65.6 3.0 %collective-permute-start.17 = (f32[8,128]{1,0:T(8,128)S(1)}, f32[8,128]{1,0:T(8,128)S(1)}, u32[]{:S(2)}, u32[]{:S(2)}) collective-permute-start(f32[8,128]{1,0:T(8,128)S(1)} %add_add_fusion.1), channel_id=1, source_target_pairs={{0,96},{32,0},{64,32},{96,64},{1,97},{33,1},{65,33},{97,65},{2,98}... | collective-permute-start | bytes 12296 | tf_op jit(solution)/shard_map/ppermute | solution.py:567
  82.0 6.1 %collective-permute-start.18 = (f32[2,768,128]{2,1,0:T(8,128)}, f32[2,768,128]{2,1,0:T(8,128)S(1)}, u32[]{:S(2)}, u32[]{:S(2)}) collective-permute-start(f32[2,768,128]{2,1,0:T(8,128)} %get-tuple-element.84), channel_id=1, source_target_pairs={{0,4},{4,0},{1,5},{5,1},{2,6},{6,2},{3,7},{7,3},{8,12},{12,8},{9,1... | collective-permute-start | bytes 2359304 | tf_op jit(solution)/shard_map/ppermute | solution.py:738
  90.2 20.2 %all-to-all-start = ((f32[64,24,128]{2,1,0:T(8,128)}), f32[64,24,128]{2,1,0:T(8,128)S(1)}, u32[]{:S(2)}, u32[]{:S(2)}) async-start(f32[64,24,128]{2,1,0:T(8,128)} %bitcast.9), calls=%async_computation | async-start | bytes 1572864 | tf_op jit(solution)/shard_map/all_to_all | solution.py:739
  131.4 5.7 %collective-permute-start.19 = (f32[64,32,128]{2,1,0:T(8,128)S(1)}, f32[64,32,128]{2,1,0:T(8,128)S(1)}, u32[]{:S(2)}, u32[]{:S(2)}) collective-permute-start(f32[64,32,128]{2,1,0:T(8,128)S(1)} %all_to_all.10.half), channel_id=1, source_target_pairs={{0,4},{4,0},{1,5},{5,1},{2,6},{6,2},{3,7},{7,3},{8,12},{12,8},{9,1... | collective-permute-start | bytes 3145736 | tf_op jit(solution)/shard_map/ppermute | solution.py:742
  (7 other events, 5.8 us)

commit v2 on v1

--- a/solution.py
+++ b/solution.py
@@ -166,21 +166,31 @@
     return jnp.where(flag == 0, 1.0, 0.0)
 
 
-def krylov_kernel(place, loads, loads_behind, loads_ahead, stiff, stiff_behind, stiff_ahead, density,
+def with_rows(place, block, ahead, behind):
+    start, stop = kept_if(place[Z_FIRST]), kept_if(place[Z_LAST])
+    space = ROWS - block.shape[0] - ahead.shape[0] - behind.shape[0]
+    zeros = jnp.zeros((space, block.shape[1]), F32)
+    return jnp.concatenate([block, ahead * stop, zeros, behind * start], axis=0)
+
+
+def load_plane(place, loads, ahead, behind, d, p):
+    slot = d * loads.shape[1] + p
+    return with_rows(place, loads[d, p], ahead[slot], behind[slot])
+
+
+def krylov_kernel(place, loads, ahead, behind, stiff, stiff_ahead, stiff_behind, density,
                   first, second, sums):
-    cells = loads.shape[1]
+    planes = loads.shape[1]
+    cells = planes - 5
     low, high = kept_if(place[SLAB_FIRST]), kept_if(place[SLAB_LAST])
-
-    def load_planes(d):
-        planes = [loads_behind[d, p] * low for p in range(2)]
-        planes += [loads[d, p] for p in range(cells)]
-        return planes + [loads_ahead[d, p] * high for p in range(3)]
-
     stiff_planes = [stiff_behind[p] * low for p in range(2)]
     stiff_planes += [stiff[p] for p in range(cells)]
     stiff_planes += [stiff_ahead[p] * high for p in range(2)]
-    force = [list(plane) for plane in zip(*[load_planes(d) for d in range(3)])]
-    free = load_planes(3)
+    loaded = [
+        [load_plane(place, loads, ahead, behind, d, p) for d in range(4)] for p in range(planes)
+    ]
+    force = [plane[:3] for plane in loaded]
+    free = [plane[3] for plane in loaded]
     image = operator_planes(force, stiff_planes, free[1:-1])
     twice = operator_planes(image, stiff_planes[1:-1], free[2:-2])
     own = (force[2 : 2 + cells], image[1 : 1 + cells], twice[:cells])
@@ -258,20 +268,21 @@
     return factors, work * moments[0] / mean
 
 
-def energy_kernel(elements, place, sums, loads, loads_ahead, first, second, density, solution, slope):
+def energy_kernel(
+    elements, place, sums, loads, ahead, behind, first, second, density, solution, slope, out
+):
     rows_of = [sums[k : k + 1, :] for k in range(2 * ITERS + 1)]
     factors, compliance = krylov_steps(rows_of[: 2 * ITERS])
     volume = rows_of[2 * ITERS]
     constant = 2.0 * penalty * (volume / elements - vol_target) / elements
     scale = -3.0 * (1.0 - emin) / compliance
     wide = [jnp.concatenate([value, value], axis=1) for value in factors + [scale, constant]]
-    high = kept_if(place[SLAB_LAST])
     cells, rows, _ = density.shape
     modes = []
     for p in range(cells + 1):
         plane = []
         for d in range(3):
-            load = loads[d, p] if p < cells else loads_ahead[d, 0] * high
+            load = load_plane(place, loads, ahead, behind, d, 2 + p)
             value = wide[0] * load + wide[1] * first[d, p] + wide[2] * second[d, p]
             if p < cells:
                 solution[d, p] = value[:rows]
@@ -280,6 +291,7 @@
     for e in range(cells):
         energy = energy_of(element_modes(modes[e], modes[e + 1]))
         held = density[e]
+        out[e] = held
         slope[e] = (wide[3] * held * held * energy + wide[4]) * held * (1.0 - held)
 
 
@@ -301,8 +313,8 @@
     for d in range(4):
         field = free if d == 3 else held * load_values[d]
         loads[d] = field
-        loads_first[d] = field[:, :3]
-        loads_last[d] = field[:, rows - 2 :]
+        loads_first[d] = field[:3]
+        loads_last[d] = field[cells - 2 :]
     columns = [column_of(frequencies[k : k + 1, :]) for k in range(3)]
     half = rows // 2
     lanes = 2 * cells * half
@@ -326,35 +338,38 @@
     middle = 0.5 * w_mid[...].astype(F32)
     w_mid_half[...] = middle.astype(BF)
     w_mid_t[...] = middle.T.astype(BF)
-    line = w_out[...].astype(F32)
+    line = w_out[...].astype(F32)[None, :]
     w_column[...] = 0.5 * column_of(line)
     w_row[...] = jnp.broadcast_to(line, w_row.shape).astype(BF)
 
 
-def with_rows(stop, start, block, ahead, behind):
-    space = ROWS - block.shape[0] - ahead.shape[0] - behind.shape[0]
-    zeros = jnp.zeros((space, block.shape[1]), F32)
-    return jnp.concatenate([block, ahead * stop, zeros, behind * start], axis=0)
-
-
-def load_rows_kernel(place, loads, ahead, behind, joined, to_before, to_next):
-    start, stop = kept_if(place[Z_FIRST]), kept_if(place[Z_LAST])
-    cells = loads.shape[1]
-    for d in range(loads.shape[0]):
-        for p in range(cells):
-            block = with_rows(stop, start, loads[d, p], ahead[d, p], behind[d, p])
-            joined[d, p] = block
-            if p < to_before.shape[1]:
-                to_before[d, p] = block
-            if p >= cells - to_next.shape[1]:
-                to_next[d, p - (cells - to_next.shape[1])] = block
+def pack_kernel(place, loads, loads_ahead, loads_behind, stiff_first, stiff_last,
+                planes, to_before, to_next):
+    low, high = kept_if(place[SLAB_FIRST]), kept_if(place[SLAB_LAST])
+    cells, rows = loads.shape[1:3]
+    count = planes.shape[1]
+    for d in range(4):
+        for p in range(count):
+            if p < 2:
+                block = loads_behind[d, p] * low
+            elif p < 2 + cells:
+                block = loads[d, p - 2]
+            else:
+                block = loads_ahead[d, p - 2 - cells] * high
+            planes[d, p] = block
+            to_before[d * count + p] = block[:3]
+            to_next[d * count + p] = block[rows - 2 :]
+    for p in range(cells):
+        to_before[4 * count + p, :2, :] = stiff_first[p]
+        to_before[4 * count + p, 2:, :] = stiff_first[p, 1:]
+        to_next[4 * count + p] = stiff_last[p]
 
 
 def stiff_rows_kernel(place, stiff, ahead, behind, joined, to_before, to_next):
-    start, stop = kept_if(place[Z_FIRST]), kept_if(place[Z_LAST])
     cells = stiff.shape[0]
+    first = ahead.shape[0] - cells
     for p in range(cells):
-        block = with_rows(stop, start, stiff[p], ahead[p], behind[p])
+        block = with_rows(place, stiff[p], ahead[first + p, :2, :], behind[first + p])
         joined[p] = block
         if p < to_before.shape[0]:
             to_before[p] = block
@@ -422,7 +437,8 @@
 ):
     density, stiff = rest[4:6]
     size = density.shape[2]
-    start = pl.multiple_of(pl.program_id(0) * (8 * size), 8 * size)
+    plane = pl.program_id(0)
+    start = pl.multiple_of(plane * (8 * size), 8 * size)
     tables, weights = (x_cos, x_sin, z_cos, z_sin), (w_in, w_mid, w_column, w_row)
     line = forward_columns(tables, weights, rest[6:], [(start + 2 * size, 0, 4 * size)])
     for r in range(8):
@@ -431,8 +447,8 @@
         else:
             q = r if r < 2 else r - 4
             part = outer[0, q : q + 1, :]
-        density[0, r : r + 1, :] = part
-        stiff[0, r : r + 1, :] = stiffness_of(part)
+        density[plane, r : r + 1, :] = part
+        stiff[plane, r : r + 1, :] = stiffness_of(part)
 
 
 def back_kernel(w_mid, slope_mid, slope_in, back, *, first, span):
@@ -551,7 +567,9 @@
     return jax.ShapeDtypeStruct(shape, dtype)
 
 
-def simple(kernel, name, out_shape, place, *operands):
+def simple(kernel, name, out_shape, place, *operands, space=None):
+    if space is not None:
+        operands = [pltpu.with_memory_space_constraint(array, space) for array in operands]
     return pl.pallas_call(
         kernel,
         name=name,
@@ -598,8 +616,8 @@
         "prepare",
         [
             shaped(4, *field),
-            shaped(4, cells_x, 3, cells_z),
-            shaped(4, cells_x, 2, cells_z),
+            shaped(4, 3, cells_y, cells_z),
+            shaped(4, 2, cells_y, cells_z),
             table,
             table,
             shaped(inputs // 2, cells_z),
@@ -611,11 +629,11 @@
             shaped(16, hidden, dtype=BF),
         ],
         place, load_values, load_mask, fixed_mask, frequencies, weight_in, weight_mid,
-        weight_out[None],
+        weight_out, space=pltpu.HBM,
     )
 
-    loads_up = shifted(loads_first, "z", -1)
-    loads_down = shifted(loads_last, "z", 1)
+    loads_ahead = shifted(loads_first, SLAB, -1)
+    loads_behind = shifted(loads_last, SLAB, 1)
     weights = (w_in_t, w_mid_t, w_column, w_row)
     weight_specs = [fixed(array.shape) for array in weights]
     x_spec = (1, inputs // 2, half_rows)
@@ -645,20 +663,16 @@
         compiler_params=params(12),
         cost_estimate=cost,
     )(x_cos, x_sin, z_cos, z_sin, *weights)
-    loads_16, loads_before, loads_next = simple(
-        load_rows_kernel,
-        "load_rows",
-        [
-            shaped(4, cells_x, ROWS, cells_z),
-            shaped(4, 3, ROWS, cells_z),
-            shaped(4, 2, ROWS, cells_z),
-        ],
-        place, loads, loads_up, loads_down,
+    planes = cells_x + 5
+    slots = 4 * planes + cells_x
+    loads, rows_first, rows_last = simple(
+        pack_kernel,
+        "pack",
+        [shaped(4, planes, cells_y, cells_z), shaped(slots, 3, cells_z), shaped(slots, 2, cells_z)],
+        place, loads, loads_ahead, loads_behind, stiff_first, stiff_last,
     )
-    loads_ahead = shifted(loads_before, SLAB, -1)
-    loads_behind = shifted(loads_next, SLAB, 1)
-    stiff_up = shifted(stiff_first, "z", -1)
-    stiff_down = shifted(stiff_last, "z", 1)
+    rows_ahead = shifted(rows_first, "z", -1)
+    rows_behind = shifted(rows_last, "z", 1)
     density, stiff, *stored = pl.pallas_call(
         inner_kernel,
         name="inner",
@@ -668,8 +682,8 @@
         + weight_specs
         + [plane_spec(half_rows)]
         + [WHOLE] * 4,
-        out_specs=[plane_spec(cells_y)] * 2 + [WHOLE] * 4,
-        out_shape=[shaped(*field)] * 2 + kept,
+        out_specs=[WHOLE] * 2 + [WHOLE] * 4,
+        out_shape=[VM(field, F32)] * 2 + kept,
         input_output_aliases={9 + k: 2 + k for k in range(4)},
         compiler_params=params(12),
         cost_estimate=cost,
@@ -679,7 +693,7 @@
         stiff_rows_kernel,
         "stiff_rows",
         [shaped(cells_x, ROWS, cells_z), shaped(2, ROWS, cells_z), shaped(2, ROWS, cells_z)],
-        place, stiff, stiff_up, stiff_down,
+        place, stiff, rows_ahead, rows_behind,
     )
     stiff_ahead = shifted(stiff_before, SLAB, -1)
     stiff_behind = shifted(stiff_next, SLAB, 1)
@@ -709,13 +723,13 @@
         krylov_kernel,
         "krylov",
         [held, held, shaped(8, 128)],
-        place, loads_16, loads_behind, loads_ahead, stiff_16, stiff_behind, stiff_ahead, density,
+        place, loads, rows_ahead, rows_behind, stiff_16, stiff_ahead, stiff_behind, density,
     )
-    solution, slope = simple(
+    solution, slope, density = simple(
         functools.partial(energy_kernel, elements_total),
         "energy",
-        [shaped(3, *field), shaped(*field)],
-        place, summed(sums), loads_16, loads_ahead, first, second, density,
+        [shaped(3, *field), shaped(*field), shaped(*field)],
+        place, summed(sums), loads, rows_ahead, rows_behind, first, second, density,
     )
 
     height = hidden + inputs
@@ -727,8 +741,8 @@
         name="gradients",
         grid=(cells_x,),
         in_specs=[SCALARS, plane_spec(cells_y), pair, pair] + z_specs + [WHOLE] * 4,
-        out_specs=[fixed((groups // 2, height, 128))] * 2 + [fixed((groups, 128))],
-        out_shape=[shaped(groups // 2, height, 128)] * 2 + [shaped(groups, 128)],
+        out_specs=[WHOLE] * 2 + [fixed((groups, 128))],
+        out_shape=[VM((groups // 2, height, 128), F32)] * 2 + [shaped(groups, 128)],
         scratch_shapes=[VM((groups, height, 128), F32), VM((hidden, 128), F32)],
         compiler_params=params(20),
     )(place, slope, *tables, z_cos, z_sin, *in_vmem(hidden_in, slope_mid, back, hidden_mid))

time: 140 us -> 133 us (0.950)
  local copies, waits for them, and re-layouts: 6.81 us -> 0.31 us
  waiting for transfers between devices: 23.9 us -> 27.5 us
  starting transfers between devices: 42.5 us -> 40.6 us
    unnamed x20 -> x10, local copies, waits for them, and re-layouts: 5.85 us -> 0.03 us
    ppermute x17 -> x15, starting transfers between devices: 23.9 us -> 19.7 us  [shifted(): lax.ppermute(block, axis, [(i, (i + distance) % size) for i in range(size)])]
    ppermute x17 -> x15, waiting for transfers between devices: 4.25 us -> 7.96 us  [shifted(): lax.ppermute(block, axis, [(i, (i + distance) % size) for i in range(size)])]
    all_to_all x1, starting transfers between devices: 5.62 us -> 8.31 us  [on_device(): share = jnp.sum(lax.all_to_all(half, CHIPS, 0, 0), axis=0)]
  transfers between devices with their start and end apart: 21 -> 19, of which waited for: 9 -> 8; matrix products, arithmetic and copies ran while one was open for 0% -> 0% of each run, Pallas kernels for 16% -> 15%
where the time goes in v2:
time: 133 us
  Pallas kernels  41.7 us (31%)
  starting transfers between devices  40.6 us (31%)
  waiting for transfers between devices  27.5 us (21%)
  blocking collectives  20.8 us (16%)
    all_to_all x1, blocking collectives, on_device(): lax.all_to_all(jnp.broadcast_to(share[None], (chips,) + share.shape), CHI...  20.8 us
    ppermute x15, starting transfers between devices, shifted(): lax.ppermute(block, axis, [(i, (i + distance) % size) for i in range(size)])  19.7 us
    all_to_all x1, waiting for transfers between devices, on_device(): share = jnp.sum(lax.all_to_all(half, CHIPS, 0, 0), axis=0)  14.5 us
    pallas_call x1, Pallas kernels, on_device(): pl.pallas_call(functools.partial(gradient_kernel, steps=cells_x), name='g...  11.5 us
    pallas_call x6, Pallas kernels, simple(): pl.pallas_call(kernel, name=name, in_specs=[SCALARS] + [WHOLE] * len(oper...  9.67 us
    all_to_all x1, starting transfers between devices, on_device(): share = jnp.sum(lax.all_to_all(half, CHIPS, 0, 0), axis=0)  8.31 us
    ppermute x15, waiting for transfers between devices, shifted(): lax.ppermute(block, axis, [(i, (i + distance) % size) for i in range(size)])  7.96 us
    pallas_call x1, Pallas kernels, on_device(): pl.pallas_call(inner_kernel, name='inner', grid=(cells_x,), in_specs=[pl....  7.33 us
  transfers between devices with their start and end apart: 19, of which 8 were waited for; matrix products, arithmetic and copies ran while one was open for 0% of the time, Pallas kernels for 15%

profile of v2, /device:TPU:1, one launch (start us, length us, event | category | flops | bytes accessed | tf_op | source)
XLA Modules:
  0.0 132.9 jit_solution(2572122772901459153)
XLA Ops:
  0.7 2.6 %prepare.1 = (f32[4,4,8,256]{3,2,1,0:T(8,128)S(1)}, f32[4,3,8,256]{3,2,1,0:T(8,128)S(1)}, f32[4,2,8,256]{3,2,1,0:T(8,128)S(1)}, f32[8,128,4]{2,1,0:T(8,128)S(1)}...) custom-call(s32[8]{0:T(128)S(1)} %stack.47.place, ...), custom_call_target="tpu_custom_call" | custom-call | tf_op jit(solution)/shard_map/prepare/pallas_call | solution.py:573
  3.4 1.5 %collective-permute-start = (f32[4,3,8,256]{3,2,1,0:T(8,128)S(1)}, f32[4,3,8,256]{3,2,1,0:T(8,128)S(1)}, u32[]{:S(2)}, u32[]{:S(2)}) collective-permute-start(f32[4,3,8,256]{3,2,1,0:T(8,128)S(1)} %get-tuple-element.49), channel_id=1, source_target_pairs={{0,124},{4,0},{8,4},{12,8},{16,12},{20,16},{24,20},{28,24},{32,28}... | collective-permute-start | bytes 294920 | tf_op jit(solution)/shard_map/ppermute | solution.py:585
  6.2 7.3 %outer.1 = (f32[4,4,256]{2,1,0:T(4,128)S(1)}, f32[4,2,256]{2,1,0:T(2,128)S(1)}, f32[4,2,256]{2,1,0:T(2,128)S(1)}, bf16[512,8192]{1,0:T(8,128)(2,1)S(1)}, bf16[51...) custom-call(f32[8,128,4]{2,1,0:T(8,128)S(1)} %get-tuple-element.51.x_cos, ...), custom_call_target="tpu_custom_call" | custom-call | flops 3221225472 | bytes 16777216 | tf_op jit(solution)/shard_map/outer/pallas_call | solution.py:651
  14.1 3.8 %collective-permute-start.2 = (f32[40,3,256]{2,1,0:T(4,128)S(1)}, f32[40,3,256]{2,1,0:T(4,128)S(1)}, u32[]{:S(2)}, u32[]{:S(2)}) collective-permute-start(f32[40,3,256]{2,1,0:T(4,128)S(1)} %get-tuple-element.62), channel_id=1, source_target_pairs={{0,3},{1,0},{2,1},{3,2},{4,7},{5,4},{6,5},{7,6},{8,11},{9,8},{10,9... | collective-permute-start | bytes 368648 | tf_op jit(solution)/shard_map/ppermute | solution.py:585
  18.0 7.3 %inner.1 = (f32[4,8,256]{2,1,0:T(8,128)S(1)}, f32[4,8,256]{2,1,0:T(8,128)S(1)}, bf16[512,8192]{1,0:T(8,128)(2,1)S(1)}, bf16[512,8192]{1,0:T(8,128)(2,1)S(1)}, bf...) custom-call(f32[8,128,4]{2,1,0:T(8,128)S(1)} %get-tuple-element.51.x, ...), custom_call_target="tpu_custom_call", output_to_operand_aliasing={{2}: (9, {}), {3}: (10, {}), {4}: (11, {}), {5}: (12, {})} | custom-call | flops 3221225472 | bytes 16777216 | tf_op jit(solution)/shard_map/inner/pallas_call | solution.py:676
  25.9 3.7 %collective-permute-start.4 = (f32[2,16,256]{2,1,0:T(8,128)S(1)}, f32[2,16,256]{2,1,0:T(8,128)S(1)}, u32[]{:S(2)}, u32[]{:S(2)}) collective-permute-start(f32[2,16,256]{2,1,0:T(8,128)S(1)} %get-tuple-element.71), channel_id=1, source_target_pairs={{0,124},{4,0},{8,4},{12,8},{16,12},{20,16},{24,20},{28,24},{32,28}... | collective-permute-start | bytes 98312 | tf_op jit(solution)/shard_map/ppermute | solution.py:585
  30.5 4.6 %collective-permute-done.5.stiff_behind = f32[2,16,256]{2,1,0:T(8,128)S(1)} collective-permute-done((f32[2,16,256]{2,1,0:T(8,128)S(1)}, f32[2,16,256]{2,1,0:T(8,128)S(1)}, u32[]{:S(2)}, u32[]{:S(2)}) %collective-permute-start.5) | collective-permute-done | bytes 32800 | tf_op jit(solution)/shard_map/ppermute | solution.py:585
  35.1 2.7 %krylov.1 = (f32[3,5,16,256]{3,2,1,0:T(8,128)S(1)}, f32[3,5,16,256]{3,2,1,0:T(8,128)S(1)}, f32[8,128]{1,0:T(8,128)S(1)}) custom-call(s32[8]{0:T(128)S(1)} %stack.47.place, f32[4,9,8,256]{3,2,1,0:T(8,128)S(1)} %get-tuple-element.61.loads, f32[40,3,256]{2,1,0:T(4,128)S(1)} %collective-permute-done.2.ahead, f32[40,2,256]{2,1,0:T(2,128)S(1)} %collective-permute-done.3.behind, ...), custom_call_target="tpu_custom_call" | custom-call | tf_op jit(solution)/shard_map/krylov/pallas_call | solution.py:573
  37.8 6.0 %collective-permute-start.6 = (f32[8,128]{1,0:T(8,128)S(1)}, f32[8,128]{1,0:T(8,128)S(1)}, u32[]{:S(2)}, u32[]{:S(2)}) collective-permute-start(f32[8,128]{1,0:T(8,128)S(1)} %get-tuple-element.74), channel_id=1, source_target_pairs={{0,4},{4,0},{1,5},{5,1},{2,6},{6,2},{3,7},{7,3},{8,12},{12,8},{9,1... | collective-permute-start | bytes 12296 | tf_op jit(solution)/shard_map/ppermute | solution.py:589
  44.6 3.9 %collective-permute-start.8 = (f32[8,128]{1,0:T(8,128)S(1)}, f32[8,128]{1,0:T(8,128)S(1)}, u32[]{:S(2)}, u32[]{:S(2)}) collective-permute-start(f32[8,128]{1,0:T(8,128)S(1)} %add.41), channel_id=1, source_target_pairs={{0,2},{1,3},{2,0},{3,1},{4,6},{5,7},{6,4},{7,5},{8,10},{9,11},{10,... | collective-permute-start | bytes 12296 | tf_op jit(solution)/shard_map/ppermute | solution.py:585
  51.0 2.6 %collective-permute-start.12 = (f32[8,128]{1,0:T(8,128)S(1)}, f32[8,128]{1,0:T(8,128)S(1)}, u32[]{:S(2)}, u32[]{:S(2)}) collective-permute-start(f32[8,128]{1,0:T(8,128)S(1)} %add_add_fusion.2), channel_id=1, source_target_pairs={{0,24},{8,0},{16,8},{24,16},{1,25},{9,1},{17,9},{25,17},{2,26},{10... | collective-permute-start | bytes 12296 | tf_op jit(solution)/shard_map/ppermute | solution.py:585
  53.6 2.9 %back_0.1.slope_in = bf16[512,8192]{1,0:T(8,128)(2,1)S(1)} custom-call(bf16[512,512]{1,0:T(8,128)(2,1)S(1)} %get-tuple-element.82.w_mid, bf16[512,8192]{1,0:T(8,128)(2,1)S(1)} %get-tuple-element.81.slope_mid, bf16[512,8192]{1,0:T(8,128)(2,1)S(1)} %get-tuple-element.83.slope_in), custom_call_target="tpu_custom_call", output_to_operand_aliasing={{}: (2, {})} | custom-call | flops 2147483648 | bytes 12582912 | tf_op jit(solution)/shard_map/back_0/pallas_call | solution.py:705
  56.8 2.6 %collective-permute-start.15 = (f32[8,128]{1,0:T(8,128)S(1)}, f32[8,128]{1,0:T(8,128)S(1)}, u32[]{:S(2)}, u32[]{:S(2)}) collective-permute-start(f32[8,128]{1,0:T(8,128)S(1)} %add_add_fusion.1), channel_id=1, source_target_pairs={{0,96},{32,0},{64,32},{96,64},{1,97},{33,1},{65,33},{97,65},{2,98}... | collective-permute-start | bytes 12296 | tf_op jit(solution)/shard_map/ppermute | solution.py:585
  59.4 2.9 %back_1.1.back = bf16[512,8192]{1,0:T(8,128)(2,1)S(1)} custom-call(bf16[512,512]{1,0:T(8,128)(2,1)S(1)} %get-tuple-element.82.w_mid, bf16[512,8192]{1,0:T(8,128)(2,1)S(1)} %get-tuple-element.81.slope_mid, bf16[512,8192]{1,0:T(8,128)(2,1)S(1)} %back_0.1.slope_in), custom_call_target="tpu_custom_call", output_to_operand_aliasing={{}: (2, {})} | custom-call | flops 2147483648 | bytes 12582912 | tf_op jit(solution)/shard_map/back_1/pallas_call | solution.py:705
  62.4 1.4 %energy.1 = (f32[3,4,8,256]{3,2,1,0:T(8,128)}, f32[4,8,256]{2,1,0:T(8,128)S(1)}, f32[4,8,256]{2,1,0:T(8,128)}) custom-call(s32[8]{0:T(128)S(1)} %stack.47.place, f32[8,128]{1,0:T(8,128)S(1)} %add_add_fusion.sums, f32[4,9,8,256]{3,2,1,0:T(8,128)S(1)} %get-tuple-element.61.loads, f32[40,3,256]{2,1,0:T(4,128)S(1)} %collective-permute-done.2.ahead, ...), custom_call_target="tpu_custom_call" | custom-call | tf_op jit(solution)/shard_map/energy/pallas_call | solution.py:573
  63.8 11.5 %gradients.1 = (f32[2,768,128]{2,1,0:T(8,128)S(1)}, f32[2,768,128]{2,1,0:T(8,128)S(1)}, f32[4,128]{1,0:T(4,128)S(1)}) custom-call(s32[8]{0:T(128)S(1)} %stack.47.place, f32[4,8,256]{2,1,0:T(8,128)S(1)} %get-tuple-element.79.slope, f32[2,4,128,4]{3,2,1,0:T(8,128)} %bitcast.13, f32[2,4,128,4]{3,2,1,0:T(8,128)} %bitcast.14, ...), custom_call_target="tpu_custom_call" | custom-call | tf_op jit(solution)/shard_map/gradients/pallas_call | solution.py:739
  75.3 3.2 %collective-permute-start.16 = (f32[2,768,128]{2,1,0:T(8,128)S(1)}, f32[2,768,128]{2,1,0:T(8,128)S(1)}, u32[]{:S(2)}, u32[]{:S(2)}) collective-permute-start(f32[2,768,128]{2,1,0:T(8,128)S(1)} %get-tuple-element.86), channel_id=1, source_target_pairs={{0,4},{4,0},{1,5},{5,1},{2,6},{6,2},{3,7},{7,3},{8,12},{12,8},{9,1... | collective-permute-start | bytes 2359304 | tf_op jit(solution)/shard_map/ppermute | solution.py:752
  78.5 1.9 %collective-permute-done.16 = f32[2,768,128]{2,1,0:T(8,128)S(1)} collective-permute-done((f32[2,768,128]{2,1,0:T(8,128)S(1)}, f32[2,768,128]{2,1,0:T(8,128)S(1)}, u32[]{:S(2)}, u32[]{:S(2)}) %collective-permute-start.16) | collective-permute-done | bytes 786464 | tf_op jit(solution)/shard_map/ppermute | solution.py:752
  81.4 8.3 %all-to-all-start = ((f32[64,24,128]{2,1,0:T(8,128)}), f32[64,24,128]{2,1,0:T(8,128)S(1)}, u32[]{:S(2)}, u32[]{:S(2)}) async-start(f32[64,24,128]{2,1,0:T(8,128)} %bitcast.9), calls=%async_computation | async-start | bytes 1572864 | tf_op jit(solution)/shard_map/all_to_all | solution.py:753
  89.8 14.5 %all-to-all-done = f32[64,24,128]{2,1,0:T(8,128)S(1)} async-done(((f32[64,24,128]{2,1,0:T(8,128)}), f32[64,24,128]{2,1,0:T(8,128)S(1)}, u32[]{:S(2)}, u32[]{:S(2)}) %all-to-all-start) | async-done | bytes 786464 | tf_op jit(solution)/shard_map/all_to_all | solution.py:753
  104.6 20.8 %all_to_all.10.half = f32[64,32,128]{2,1,0:T(8,128)S(1)} all-to-all(f32[64,32,128]{2,1,0:T(8,128)S(1)} %broadcast_in_dim.10), channel_id=1, replica_groups=mesh['x'=4,'y'=4,'c'=2,'z'=4] {'x','y','z'}, dimensions={0} | all-to-all | bytes 2097152 | tf_op jit(solution)/shard_map/all_to_all | solution.py:755
  125.3 3.5 %collective-permute-start.17 = (f32[64,32,128]{2,1,0:T(8,128)S(1)}, f32[64,32,128]{2,1,0:T(8,128)S(1)}, u32[]{:S(2)}, u32[]{:S(2)}) collective-permute-start(f32[64,32,128]{2,1,0:T(8,128)S(1)} %all_to_all.10.half), channel_id=1, source_target_pairs={{0,4},{4,0},{1,5},{5,1},{2,6},{6,2},{3,7},{7,3},{8,12},{12,8},{9,1... | collective-permute-start | bytes 3145736 | tf_op jit(solution)/shard_map/ppermute | solution.py:756
  128.8 2.3 %collective-permute-done.17.away = f32[64,32,128]{2,1,0:T(8,128)S(1)} collective-permute-done((f32[64,32,128]{2,1,0:T(8,128)S(1)}, f32[64,32,128]{2,1,0:T(8,128)S(1)}, u32[]{:S(2)}, u32[]{:S(2)}) %collective-permute-start.17) | collective-permute-done | bytes 1048608 | tf_op jit(solution)/shard_map/ppermute | solution.py:756
  131.1 1.8 %finish.1 = (f32[256,512]{1,0:T(8,128)}, f32[512,512]{1,0:T(8,128)}, f32[4,128]{1,0:T(4,128)}) custom-call(s32[8]{0:T(128)S(1)} %stack.47.place, f32[64,32,128]{2,1,0:T(8,128)S(1)} %all_to_all.10.half, f32[64,32,128]{2,1,0:T(8,128)S(1)} %collective-permute-done.17.away), custom_call_target="tpu_custom_call" | custom-call | tf_op jit(solution)/shard_map/finish/pallas_call | solution.py:573
  (48 shorter events, 8.4 us)
Async XLA Ops:
  3.3 22.0 %copy-start.1 = (f32[8,128,4]{2,1,0:T(8,128)}, f32[8,128,4]{2,1,0:T(8,128)S(1)}, u32[]{:S(2)}) copy-start(f32[8,128,4]{2,1,0:T(8,128)S(1)} %get-tuple-element.51.x_cos) | copy-start | bytes 49156
  3.3 22.0 %copy-start.2 = (f32[8,128,4]{2,1,0:T(8,128)}, f32[8,128,4]{2,1,0:T(8,128)S(1)}, u32[]{:S(2)}) copy-start(f32[8,128,4]{2,1,0:T(8,128)S(1)} %get-tuple-element.52.x_sin) | copy-start | bytes 49156
  3.4 10.2 %collective-permute-start = (f32[4,3,8,256]{3,2,1,0:T(8,128)S(1)}, f32[4,3,8,256]{3,2,1,0:T(8,128)S(1)}, u32[]{:S(2)}, u32[]{:S(2)}) collective-permute-start(f32[4,3,8,256]{3,2,1,0:T(8,128)S(1)} %get-tuple-element.49), channel_id=1, source_target_pairs={{0,124},{4,0},{8,4},{12,8},{16,12},{20,16},{24,20},{28,24},{32,28}... | collective-permute-start | bytes 294920 | tf_op jit(solution)/shard_map/ppermute | solution.py:585
  4.8 8.7 %collective-permute-start.1 = (f32[4,2,8,256]{3,2,1,0:T(8,128)S(1)}, f32[4,2,8,256]{3,2,1,0:T(8,128)S(1)}, u32[]{:S(2)}, u32[]{:S(2)}) collective-permute-start(f32[4,2,8,256]{3,2,1,0:T(8,128)S(1)} %get-tuple-element.50), channel_id=1, source_target_pairs={{0,4},{4,8},{8,12},{12,16},{16,20},{20,24},{24,28},{28,32},{32,36}... | collective-permute-start | bytes 196616 | tf_op jit(solution)/shard_map/ppermute | solution.py:585
  14.1 11.2 %collective-permute-start.2 = (f32[40,3,256]{2,1,0:T(4,128)S(1)}, f32[40,3,256]{2,1,0:T(4,128)S(1)}, u32[]{:S(2)}, u32[]{:S(2)}) collective-permute-start(f32[40,3,256]{2,1,0:T(4,128)S(1)} %get-tuple-element.62), channel_id=1, source_target_pairs={{0,3},{1,0},{2,1},{3,2},{4,7},{5,4},{6,5},{7,6},{8,11},{9,8},{10,9... | collective-permute-start | bytes 368648 | tf_op jit(solution)/shard_map/ppermute | solution.py:585
  18.0 7.4 %collective-permute-start.3 = (f32[40,2,256]{2,1,0:T(2,128)S(1)}, f32[40,2,256]{2,1,0:T(2,128)S(1)}, u32[]{:S(2)}, u32[]{:S(2)}) collective-permute-start(f32[40,2,256]{2,1,0:T(2,128)S(1)} %get-tuple-element.63), channel_id=1, source_target_pairs={{0,1},{1,2},{2,3},{3,0},{4,5},{5,6},{6,7},{7,4},{8,9},{9,10},{10,1... | collective-permute-start | bytes 245768 | tf_op jit(solution)/shard_map/ppermute | solution.py:585
  25.3 31.2 %copy-start = (bf16[512,8192]{1,0:T(8,128)(2,1)}, bf16[512,8192]{1,0:T(8,128)(2,1)S(1)}, u32[]{:S(2)}) copy-start(bf16[512,8192]{1,0:T(8,128)(2,1)S(1)} %get-tuple-element.80.hidden_in) | copy-start | bytes 25165828
  25.9 4.6 %collective-permute-start.4 = (f32[2,16,256]{2,1,0:T(8,128)S(1)}, f32[2,16,256]{2,1,0:T(8,128)S(1)}, u32[]{:S(2)}, u32[]{:S(2)}) collective-permute-start(f32[2,16,256]{2,1,0:T(8,128)S(1)} %get-tuple-element.71), channel_id=1, source_target_pairs={{0,124},{4,0},{8,4},{12,8},{16,12},{20,16},{24,20},{28,24},{32,28}... | collective-permute-start | bytes 98312 | tf_op jit(solution)/shard_map/ppermute | solution.py:585
  29.6 5.5 %collective-permute-start.5 = (f32[2,16,256]{2,1,0:T(8,128)S(1)}, f32[2,16,256]{2,1,0:T(8,128)S(1)}, u32[]{:S(2)}, u32[]{:S(2)}) collective-permute-start(f32[2,16,256]{2,1,0:T(8,128)S(1)} %get-tuple-element.72), channel_id=1, source_target_pairs={{0,4},{4,8},{8,12},{12,16},{16,20},{20,24},{24,28},{28,32},{32,36}... | collective-permute-start | bytes 98312 | tf_op jit(solution)/shard_map/ppermute | solution.py:585
  37.8 6.8 %collective-permute-start.6 = (f32[8,128]{1,0:T(8,128)S(1)}, f32[8,128]{1,0:T(8,128)S(1)}, u32[]{:S(2)}, u32[]{:S(2)}) collective-permute-start(f32[8,128]{1,0:T(8,128)S(1)} %get-tuple-element.74), channel_id=1, source_target_pairs={{0,4},{4,0},{1,5},{5,1},{2,6},{6,2},{3,7},{7,3},{8,12},{12,8},{9,1... | collective-permute-start | bytes 12296 | tf_op jit(solution)/shard_map/ppermute | solution.py:589
  44.6 3.9 %collective-permute-start.7 = (f32[8,128]{1,0:T(8,128)S(1)}, f32[8,128]{1,0:T(8,128)S(1)}, u32[]{:S(2)}, u32[]{:S(2)}) collective-permute-start(f32[8,128]{1,0:T(8,128)S(1)} %add.41), channel_id=1, source_target_pairs={{0,1},{1,2},{2,3},{3,0},{4,5},{5,6},{6,7},{7,4},{8,9},{9,10},{10,1... | collective-permute-start | bytes 12296 | tf_op jit(solution)/shard_map/ppermute | solution.py:585
  44.6 4.9 %collective-permute-start.8 = (f32[8,128]{1,0:T(8,128)S(1)}, f32[8,128]{1,0:T(8,128)S(1)}, u32[]{:S(2)}, u32[]{:S(2)}) collective-permute-start(f32[8,128]{1,0:T(8,128)S(1)} %add.41), channel_id=1, source_target_pairs={{0,2},{1,3},{2,0},{3,1},{4,6},{5,7},{6,4},{7,5},{8,10},{9,11},{10,... | collective-permute-start | bytes 12296 | tf_op jit(solution)/shard_map/ppermute | solution.py:585
  48.5 2.5 %collective-permute-start.9 = (f32[8,128]{1,0:T(8,128)S(1)}, f32[8,128]{1,0:T(8,128)S(1)}, u32[]{:S(2)}, u32[]{:S(2)}) collective-permute-start(f32[8,128]{1,0:T(8,128)S(1)} %add.41), channel_id=1, source_target_pairs={{0,3},{1,0},{2,1},{3,2},{4,7},{5,4},{6,5},{7,6},{8,11},{9,8},{10,9... | collective-permute-start | bytes 12296 | tf_op jit(solution)/shard_map/ppermute | solution.py:585
  50.9 5.6 %collective-permute-start.10 = (f32[8,128]{1,0:T(8,128)S(1)}, f32[8,128]{1,0:T(8,128)S(1)}, u32[]{:S(2)}, u32[]{:S(2)}) collective-permute-start(f32[8,128]{1,0:T(8,128)S(1)} %add_add_fusion.2), channel_id=1, source_target_pairs={{0,8},{8,16},{16,24},{24,0},{1,9},{9,17},{17,25},{25,1},{2,10},{10... | collective-permute-start | bytes 12296 | tf_op jit(solution)/shard_map/ppermute | solution.py:585
  50.9 5.6 %collective-permute-start.11 = (f32[8,128]{1,0:T(8,128)S(1)}, f32[8,128]{1,0:T(8,128)S(1)}, u32[]{:S(2)}, u32[]{:S(2)}) collective-permute-start(f32[8,128]{1,0:T(8,128)S(1)} %add_add_fusion.2), channel_id=1, source_target_pairs={{0,16},{8,24},{16,0},{24,8},{1,17},{9,25},{17,1},{25,9},{2,18},{10... | collective-permute-start | bytes 12296 | tf_op jit(solution)/shard_map/ppermute | solution.py:585
  51.0 5.6 %collective-permute-start.12 = (f32[8,128]{1,0:T(8,128)S(1)}, f32[8,128]{1,0:T(8,128)S(1)}, u32[]{:S(2)}, u32[]{:S(2)}) collective-permute-start(f32[8,128]{1,0:T(8,128)S(1)} %add_add_fusion.2), channel_id=1, source_target_pairs={{0,24},{8,0},{16,8},{24,16},{1,25},{9,1},{17,9},{25,17},{2,26},{10... | collective-permute-start | bytes 12296 | tf_op jit(solution)/shard_map/ppermute | solution.py:585
  56.6 7.2 %slice-start = ((s8[8388608]{0:T(1024)(128)(4,1)}), s8[4194304]{0:T(1024)(128)(4,1)S(1)}, s32[]{:S(2)}) async-start(s8[8388608]{0:T(1024)(128)(4,1)} %bitcast.11), calls=%async_computation.2 | async-start | bytes 8388608
  56.6 7.2 %slice-start.1 = ((s8[8388608]{0:T(1024)(128)(4,1)}), s8[4194304]{0:T(1024)(128)(4,1)S(1)}, s32[]{:S(2)}) async-start(s8[8388608]{0:T(1024)(128)(4,1)} %bitcast.11), calls=%async_computation.3 | async-start | bytes 8388608
  56.6 5.7 %collective-permute-start.13 = (f32[8,128]{1,0:T(8,128)S(1)}, f32[8,128]{1,0:T(8,128)S(1)}, u32[]{:S(2)}, u32[]{:S(2)}) collective-permute-start(f32[8,128]{1,0:T(8,128)S(1)} %add_add_fusion.1), channel_id=1, source_target_pairs={{0,32},{32,64},{64,96},{96,0},{1,33},{33,65},{65,97},{97,1},{2,34}... | collective-permute-start | bytes 12296 | tf_op jit(solution)/shard_map/ppermute | solution.py:585
  56.7 5.6 %collective-permute-start.14 = (f32[8,128]{1,0:T(8,128)S(1)}, f32[8,128]{1,0:T(8,128)S(1)}, u32[]{:S(2)}, u32[]{:S(2)}) collective-permute-start(f32[8,128]{1,0:T(8,128)S(1)} %add_add_fusion.1), channel_id=1, source_target_pairs={{0,64},{32,96},{64,0},{96,32},{1,65},{33,97},{65,1},{97,33},{2,66}... | collective-permute-start | bytes 12296 | tf_op jit(solution)/shard_map/ppermute | solution.py:585
  56.8 5.5 %collective-permute-start.15 = (f32[8,128]{1,0:T(8,128)S(1)}, f32[8,128]{1,0:T(8,128)S(1)}, u32[]{:S(2)}, u32[]{:S(2)}) collective-permute-start(f32[8,128]{1,0:T(8,128)S(1)} %add_add_fusion.1), channel_id=1, source_target_pairs={{0,96},{32,0},{64,32},{96,64},{1,97},{33,1},{65,33},{97,65},{2,98}... | collective-permute-start | bytes 12296 | tf_op jit(solution)/shard_map/ppermute | solution.py:585
  75.3 5.1 %collective-permute-start.16 = (f32[2,768,128]{2,1,0:T(8,128)S(1)}, f32[2,768,128]{2,1,0:T(8,128)S(1)}, u32[]{:S(2)}, u32[]{:S(2)}) collective-permute-start(f32[2,768,128]{2,1,0:T(8,128)S(1)} %get-tuple-element.86), channel_id=1, source_target_pairs={{0,4},{4,0},{1,5},{5,1},{2,6},{6,2},{3,7},{7,3},{8,12},{12,8},{9,1... | collective-permute-start | bytes 2359304 | tf_op jit(solution)/shard_map/ppermute | solution.py:752
  81.4 22.9 %all-to-all-start = ((f32[64,24,128]{2,1,0:T(8,128)}), f32[64,24,128]{2,1,0:T(8,128)S(1)}, u32[]{:S(2)}, u32[]{:S(2)}) async-start(f32[64,24,128]{2,1,0:T(8,128)} %bitcast.9), calls=%async_computation | async-start | bytes 1572864 | tf_op jit(solution)/shard_map/all_to_all | solution.py:753
  125.3 5.7 %collective-permute-start.17 = (f32[64,32,128]{2,1,0:T(8,128)S(1)}, f32[64,32,128]{2,1,0:T(8,128)S(1)}, u32[]{:S(2)}, u32[]{:S(2)}) collective-permute-start(f32[64,32,128]{2,1,0:T(8,128)S(1)} %all_to_all.10.half), channel_id=1, source_target_pairs={{0,4},{4,0},{1,5},{5,1},{2,6},{6,2},{3,7},{7,3},{8,12},{12,8},{9,1... | collective-permute-start | bytes 3145736 | tf_op jit(solution)/shard_map/ppermute | solution.py:756
